TPU v7x, 128 devices: a whole 4x4x4 slice. The times are simulated.
128 devices in a mesh: wide: 16 (over x_lo, y, core), narrow: 8 (over x_hi, z).
Axes of the slice: x: 4 (x_hi: 2, x_lo: 2; x = x_hi * 2 + x_lo), y: 4, z: 4, core: 2. Of those that a mesh axis runs over, the one named last changes fastest.
Arguments:
- base: float32 [1, 16, 2, 8, 512, 512], P(None, 'wide', None, 'narrow'), may hold values from -3.7 to 8
- block_mask: int32 [16, 16], replicated, may hold values 0 or 1
- heads: float32 [8192], P('narrow'), may hold values from -6 to 6
- coef: float32 [9000], replicated, may hold values from 0.3 to 1.2
- weir_node: int32 [9000], replicated, may hold values from 0 to 4095
- weir_cell: int32 [9000], replicated, may hold values from 4096 to 8191
Outputs:
- factored: float32 [1, 16, 2, 8, 512, 512], P(None, 'wide', None, 'narrow')
All inputs are finite; a program needn't handle non-finite values.
Results may differ from a plain program's by a relative error of at most 0.0001.
Values sent between devices are 32-bit elements; how exact they have to be, the bound alone decides.
A program may use at most 64 MiB of HBM per device.

v0:
```python
import jax
import jax.numpy as jnp
from jax import lax
from jax.sharding import PartitionSpec as P

PANELS = 2
NS_STEPS = 6


def spread(shard, axis, root):
    mine = lax.axis_index(axis) == root
    return lax.psum(jnp.where(mine, shard, jnp.zeros_like(shard)), axis)


def newton_schulz(block):
    approx = jnp.diag(1.0 / jnp.diagonal(block))
    for step in range(NS_STEPS):
        inner = jnp.dot(block, approx, precision=lax.Precision.HIGHEST)
        approx = 2.0 * approx - jnp.dot(approx, inner, precision=lax.Precision.HIGHEST)
    return approx


def panel(blocks, step, row_id, col_id, wide, narrow, colj):
    root_row = step % wide
    root_col = step % narrow
    local_row = step // wide
    local_col = step // narrow
    in_row = row_id == root_row
    lower = spread(blocks[:, local_col], "narrow", root_col)
    owner = in_row & (col_id == root_col)
    inverse = lax.cond(owner, newton_schulz, jnp.zeros_like, blocks[local_row, local_col])
    inverse = spread(inverse, "narrow", root_col)
    scaled = jnp.einsum("pq,jqs->jps", inverse, blocks[local_row], precision=lax.Precision.HIGHEST)
    take = in_row & (colj > step)
    newrow = jnp.where(take[:, None, None], scaled, blocks[local_row])
    blocks = blocks.at[local_row].set(newrow)
    upper = spread(newrow, "wide", root_row)
    return (blocks, lower, upper)


def trailing(blocks, lower, upper, step, rowi, colj, select):
    term = jnp.einsum("aps,bsq->abpq", lower, upper, precision=lax.Precision.HIGHEST)
    keep = (rowi > step)[:, None] & (colj > step)[None, :] & select
    return jnp.where(keep[:, :, None, None], blocks - term, blocks)


def per_device(base, block_mask, heads, coef, weir_node, weir_cell):
    wide = lax.axis_size("wide")
    narrow = lax.axis_size("narrow")
    row_id = lax.axis_index("wide")
    col_id = lax.axis_index("narrow")
    nrow = base.shape[0]
    ncol = base.shape[2]
    width = base.shape[4]
    blocks = base.reshape(nrow, ncol, width, width)
    rowi = jnp.arange(nrow, dtype=jnp.int32) * wide + row_id
    colj = jnp.arange(ncol, dtype=jnp.int32) * narrow + col_id
    local_mask = block_mask[rowi[:, None], colj[None, :]]
    keep = (local_mask != 0) | (rowi[:, None] == colj[None, :])
    blocks = blocks * keep.astype(blocks.dtype)[:, :, None, None]
    every_head = lax.all_gather(heads, "narrow", axis=0, tiled=True)
    drop = every_head[weir_node] - every_head[weir_cell]
    flux = 1.5 * coef * jnp.sqrt(drop * drop + 0.01)
    rows = jnp.concatenate([weir_node, weir_cell, weir_node, weir_cell])
    cols = jnp.concatenate([weir_node, weir_cell, weir_cell, weir_node])
    vals = jnp.concatenate([flux, flux, -flux, -flux])
    block_row = rows // width
    block_col = cols // width
    owned = (block_row % wide == row_id) & (block_col % narrow == col_id)
    place_row = jnp.where(owned, block_row // wide, nrow)
    place_col = block_col // narrow
    blocks = blocks.at[place_row, place_col, rows % width, cols % width].add(vals, mode="drop")
    everything = jnp.ones((nrow, ncol), bool)
    for step in range(PANELS):
        blocks, lower, upper = panel(blocks, step, row_id, col_id, wide, narrow, colj)
        blocks = trailing(blocks, lower, upper, step, rowi, colj, everything)
    return blocks.reshape(base.shape)


def solution(mesh):
    placed = (P(None, "wide", None, "narrow", None, None), P(), P("narrow"), P(), P(), P())
    return jax.shard_map(
        per_device,
        mesh=mesh,
        in_specs=placed,
        out_specs=P(None, "wide", None, "narrow", None, None),
        check_vma=False,
    )
```

profile of v0, /device:TPU:21, one launch (start us, length us, event | category | flops | bytes accessed | tf_op | source)
XLA Modules:
  0.0 873.0 jit_solution(4752694818298976993)
XLA Ops:
  16.8 3.4 compare_select_fusion.3
  24.9 27.7 %all_gather.3 = f32[8192]{0:T(1024)S(1)} all-gather(f32[1024]{0:T(1024)S(1)} %copy-done.7), channel_id=1, replica_groups=mesh['wide'=16,'narrow'=8] {'narrow'}, dimensions={0}, use_global_device_ids=true | all-gather | bytes 36864 | tf_op jit(solution)/shard_map/all_gather | solution.py:61
  52.7 46.7 %gather_fusion.3 = f32[9000]{0:T(1024)S(1)} fusion(f32[8192]{0:T(1024)S(1)} %all_gather.3, s32[9216]{0:T(1024)S(1)} %pad_clamp_fusion.1), kind=kCustom, calls=%fused_computation.3 | custom fusion | bytes 108000 | tf_op jit(solution)/shard_map/gather | solution.py:62
  99.4 46.7 %gather_fusion.4 = f32[9000]{0:T(1024)S(1)} fusion(f32[8192]{0:T(1024)S(1)} %all_gather.3, s32[9216]{0:T(1024)S(1)} %pad_clamp_fusion), kind=kCustom, calls=%fused_computation.4 | custom fusion | bytes 108000 | tf_op jit(solution)/shard_map/gather | solution.py:62
  146.3 190.0 %scatter_fusion = f32[524288]{0:T(1024)S(1)} fusion(f32[524288]{0:T(1024)S(1)} %bitcast.129, s32[36000]{0:T(1024)S(1)} %broadcast_select_fusion.4, f32[36000]{0:T(1024)S(1)} %concatenate.125), kind=kCustom, calls=%fused_computation.5 | custom fusion | flops 36000 | bytes 576000
  336.3 1.5 reshape.1128
  337.8 2.3 slice.70
  340.1 1.6 copy.35
  341.7 1.1 select_bitcast_fusion.1
  342.8 6.8 conditional.2
  350.8 1.5 squeeze.22
  352.3 3.1 copy.23
  355.3 108.6 %all-reduce.14.cloned.1.call-done = (f32[512,512]{1,0:T(8,128)}, f32[512,512]{0,1:T(8,128)}) async-done(((f32[512,512]{1,0:T(8,128)}, f32[512,512]{0,1:T(8,128)}), (f32[512,512]{1,0:T(8,128)}, f32[512,512]{0,1:T(8,128)})) %all-reduce.14.cloned.1.call-update) | async-done | bytes 2097168 | tf_op jit(solution)/shard_map/psum | solution.py:12
  463.9 10.1 %broadcast_select_fusion.1 = (f32[2,512,512]{1,2,0:T(8,128)}, f32[2,512,512]{1,2,0:T(8,128)}) fusion(pred[]{:T(512)S(6)} %eq.71, f32[2,512,512]{1,2,0:T(8,128)} %copy.23, f32[2,512,512]{2,1,0:T(8,128)S(1)} %copy-done.2, f32[512,512]{1,0:T(8,128)} %get-tuple-element.43, pred[2]{0:T(512)(128)(4,1)S(1)} %compare_and_fusion), kind=kOutput, calls=%fused_computation.83 | convolution fusion | flops 3222274048 | bytes 9437187 | tf_op jit(solution)/shard_map/pq,jqs->jps/dot_general | solution.py:33
  474.1 127.2 %all-reduce.8.cloned.1.call-done = f32[2,512,512]{1,2,0:T(8,128)} async-done(((f32[2,512,512]{1,2,0:T(8,128)}), f32[2,512,512]{1,2,0:T(8,128)}) %all-reduce.8.cloned.1.call-update) | async-done | bytes 2097168 | tf_op jit(solution)/shard_map/psum | solution.py:12
  601.3 5.8 subtract_select_fusion.1
  607.1 1.3 select_bitcast_fusion
  608.3 4.9 conditional.3
  613.3 1.1 broadcast_select_fusion.2
  614.4 110.2 %all-reduce.12.cloned.1.call-done = (f32[512,512]{1,0:T(8,128)}, f32[512,512]{0,1:T(8,128)}) async-done(((f32[512,512]{1,0:T(8,128)}, f32[512,512]{0,1:T(8,128)}), (f32[512,512]{1,0:T(8,128)}, f32[512,512]{0,1:T(8,128)})) %all-reduce.12.cloned.1.call-update) | async-done | bytes 2097168 | tf_op jit(solution)/shard_map/psum | solution.py:12
  724.7 6.4 broadcast_select_fusion
  731.1 127.3 %all-reduce.10.cloned.1.call-done = f32[2,512,512]{1,2,0:T(8,128)} async-done(((f32[2,512,512]{1,2,0:T(8,128)}), f32[2,512,512]{1,2,0:T(8,128)}) %all-reduce.10.cloned.1.call-update) | async-done | bytes 2097168 | tf_op jit(solution)/shard_map/psum | solution.py:12
  858.4 5.8 fusion.48
  864.2 1.8 copy.27
  (64 shorter events, 16.5 us)
Async XLA Ops:
  6.5 16.8 %copy-start = (s32[16,16]{1,0:T(8,128)S(1)}, s32[16,16]{1,0:T(8,128)}, u32[]{:S(2)}) copy-start(s32[16,16]{1,0:T(8,128)} %param.15) | copy-start | bytes 3076
  6.5 14.7 %copy-start.8 = (s32[4]{0:T(128)S(1)}, s32[4]{0:T(128)}, u32[]{:S(2)}) copy-start(s32[4]{0:T(128)} %constant.189) | copy-start | bytes 52
  6.5 15.6 %copy-start.9 = (s32[4]{0:T(128)S(1)}, s32[4]{0:T(128)}, u32[]{:S(2)}) copy-start(s32[4]{0:T(128)} %constant.192) | copy-start | bytes 52
  6.5 457.3 %all-reduce.14.cloned.1.call-start = ((), (), s32[]{:S(2)}) async-start(), calls=%async_computation.3 | async-start | bytes 4194304 | tf_op jit(solution)/shard_map/psum | solution.py:12
  7.4 16.6 %copy-start.3 = (f32[1,1,2,1,512,512]{5,4,3,2,1,0:T(8,128)S(1)}, f32[1,1,2,1,512,512]{5,4,3,2,1,0:T(8,128)}, u32[]{:S(2)}) copy-start(f32[1,1,2,1,512,512]{5,4,3,2,1,0:T(8,128)} %param.14) | copy-start | bytes 6291460
  24.2 0.7 copy-start.7
  99.4 46.8 %copy-start.6 = (f32[9000]{0:T(1024)S(1)}, f32[9000]{0:T(1024)}, u32[]{:S(2)}) copy-start(f32[9000]{0:T(1024)} %param.17) | copy-start | bytes 108004
  350.7 250.6 %all-reduce.8.cloned.1.call-start = ((), (), s32[]{:S(2)}) async-start(), calls=%async_computation | async-start | bytes 4194304 | tf_op jit(solution)/shard_map/psum | solution.py:12
  352.2 111.6 %copy-start.2 = (f32[2,512,512]{2,1,0:T(8,128)S(1)}, f32[2,512,512]{2,1,0:T(8,128)}, u32[]{:S(2)}) copy-start(f32[2,512,512]{2,1,0:T(8,128)} %squeeze.22) | copy-start | bytes 6291460
  474.0 127.3 %copy-start.4 = (f32[512,512]{0,1:T(8,128)S(1)}, f32[512,512]{0,1:T(8,128)}, u32[]{:S(2)}) copy-start(f32[512,512]{0,1:T(8,128)} %get-tuple-element.44) | copy-start | bytes 3145732
  474.0 250.7 %all-reduce.12.cloned.1.call-start = ((), (), s32[]{:S(2)}) async-start(), calls=%async_computation.2 | async-start | bytes 4194304 | tf_op jit(solution)/shard_map/psum | solution.py:12
  614.4 244.0 %all-reduce.10.cloned.1.call-start = ((), (), s32[]{:S(2)}) async-start(), calls=%async_computation.1 | async-start | bytes 4194304 | tf_op jit(solution)/shard_map/psum | solution.py:12
  731.1 127.3 %copy-start.5 = (f32[512,512]{0,1:T(8,128)S(1)}, f32[512,512]{0,1:T(8,128)}, u32[]{:S(2)}) copy-start(f32[512,512]{0,1:T(8,128)} %get-tuple-element.42) | copy-start | bytes 3145732
  858.4 7.6 copy-start.1
Sparse Core Ops, SparseCore 0:
  350.8 113.0 all-reduce.13
  474.2 127.1 all-reduce.7
  614.5 110.1 all-reduce.11
  731.2 127.1 all-reduce.9
where the time goes:
time: 884 us; the launch traced here: 873 us
  waiting for transfers between devices  473 us (54%)
  other arithmetic  203 us (23%)
  local copies, waits for them, and re-layouts  115 us (13%)
  matrix products  28 us (3%)
  blocking collectives  27.7 us (3%)
  between operations  13.9 us (2%)
  loops' own time  11.5 us (1%)
    psum x4, waiting for transfers between devices, spread(): return lax.psum(jnp.where(mine, shard, jnp.zeros_like(shard)), axis)  473 us
    unnamed x6, other arithmetic  192 us
    gather x2, local copies, waits for them, and re-layouts, per_device(): drop = every_head[weir_node] - every_head[weir_cell]  93.4 us
    all_gather x1, blocking collectives, per_device(): every_head = lax.all_gather(heads, 'narrow', axis=0, tiled=True)  27.7 us
  transfers between devices with their start and end apart: 4, of which 4 were waited for; matrix products, arithmetic and copies ran while one was open for 1% of the time, Pallas kernels for 0%

commit v1 on v0

v1 whole, which is shorter than its diff:
```python
import functools

import jax
import jax.numpy as jnp
from jax import lax
from jax.experimental import pallas as pl
from jax.experimental.pallas import tpu as pltpu
from jax.sharding import PartitionSpec as P

NS_STEPS = 6
B = 512
ROWS = 72
LANES = 128
MESH = pl.DeviceIdType.MESH
F32 = jnp.float32
BF16 = jnp.bfloat16
VMEM_LIMIT = 56 * 2**20
TREE_ROWS = ((0, 88), (88, 88), (176, 80))


def split(x):
    high = x.astype(BF16)
    return high, (x - high.astype(F32)).astype(BF16)


def dot(a, b):
    return jnp.dot(a, b, preferred_element_type=F32)


def dot_nt(a, b):
    return lax.dot_general(a, b, (((1,), (1,)), ((), ())), preferred_element_type=F32)


def product(ah, al, bh, bl):
    return dot(ah, bh) + dot(ah, bl) + dot(al, bh)


def gather_heads_kernel(mine_ref, every_ref, send_sem, recv_sem):
    r = lax.axis_index("wide")
    c = lax.axis_index("narrow")
    count = 8
    barrier = pltpu.get_barrier_semaphore()
    for hop in range(1, count):
        pl.semaphore_signal(barrier, inc=1, device_id=(r, lax.rem(c + hop, count)), device_id_type=MESH)
    pl.semaphore_wait(barrier, count - 1)
    place = pl.ds(pl.multiple_of(c * 8, 8), 8)
    copies = []
    for hop in range(1, count):
        copy = pltpu.make_async_remote_copy(
            src_ref=mine_ref,
            dst_ref=every_ref.at[place],
            send_sem=send_sem.at[hop],
            recv_sem=recv_sem.at[hop],
            device_id=(r, lax.rem(c + hop, count)),
            device_id_type=MESH,
        )
        copy.start()
        copies.append(copy)
    every_ref[place] = mine_ref[...]
    for copy in copies:
        copy.wait()


def gather_heads(heads):
    return pl.pallas_call(
        gather_heads_kernel,
        out_shape=jax.ShapeDtypeStruct((64, LANES), F32),
        in_specs=[pl.BlockSpec(memory_space=pltpu.VMEM)],
        out_specs=pl.BlockSpec(memory_space=pltpu.VMEM),
        scratch_shapes=[pltpu.SemaphoreType.DMA((8,)), pltpu.SemaphoreType.DMA((8,))],
        compiler_params=pltpu.CompilerParams(collective_id=0, has_side_effects=True),
        name="gather_heads",
    )(heads.reshape(8, LANES))


def lookup(table_ref, first, index):
    high = lax.shift_right_logical(index, 7) - first
    low = jnp.bitwise_and(index, 127)
    found = jnp.zeros(index.shape, F32)
    for t in range(32):
        row = jnp.broadcast_to(table_ref[pl.ds(first + t, 1), :], index.shape)
        picked = jnp.take_along_axis(row, low, axis=1, mode="promise_in_bounds")
        found = jnp.where(high == t, picked, found)
    return found


def pieces(x):
    high = x.astype(BF16).astype(F32)
    rest = x - high
    middle = rest.astype(BF16).astype(F32)
    return high, middle, rest - middle


def weirs_kernel(mask_ref, base_ref, heads_ref, coef_ref, node_ref, cell_ref, out_ref, code_ref, flux_ref):
    r = lax.axis_index("wide")
    c = lax.axis_index("narrow")
    upper = r < 8
    for j in range(2):
        col = c + 8 * j
        keep = jnp.where((mask_ref[r, col] != 0) | (r == col), 1.0, 0.0).astype(F32)
        out_ref[j] = base_ref[j] * keep
    node = node_ref[...]
    cell = cell_ref[...]
    drop = lookup(heads_ref, 0, node) - lookup(heads_ref, 32, cell)
    flux = 1.5 * coef_ref[...] * jnp.sqrt(drop * drop + 0.01)
    row = jnp.where(upper, node, cell)
    col = jnp.where(upper, cell, node)
    mine = lax.shift_right_logical(row, 9) == r
    low_row = jnp.bitwise_and(row, 511)

    target = jnp.where(upper, c + 8, c)
    slot = jnp.where(upper, 1, 0)
    hit = jnp.where(mine & (lax.shift_right_logical(col, 9) == target), 1, 0)
    code = low_row * 512 + jnp.bitwise_and(col, 511)
    steps = jnp.max(jnp.sum(hit.astype(F32), axis=0, keepdims=True)).astype(jnp.int32)
    code_ref[...] = jnp.zeros(code_ref.shape, jnp.int32)
    flux_ref[...] = jnp.zeros(flux_ref.shape, F32)
    place = lax.broadcasted_iota(jnp.int32, (ROWS, LANES), 0)

    def extract(s, left):
        first = jnp.min(jnp.where(left != 0, place, ROWS), axis=0, keepdims=True)
        now = place == first
        code_ref[pl.ds(s, 1), :] = jnp.sum(jnp.where(now, code, 0), axis=0, keepdims=True)
        flux_ref[pl.ds(s, 1), :] = jnp.sum(jnp.where(now, flux, 0.0), axis=0, keepdims=True)
        return jnp.where(now, 0, left)

    lax.fori_loop(0, steps, extract, hit)

    def scatter(b, carry):
        rows = pl.ds(pl.multiple_of(b * 8, 8), 8)
        codes = code_ref[rows]
        parts = pieces(flux_ref[rows])
        here = lax.broadcasted_iota(jnp.int32, (B, LANES), 0)
        row_of = lax.shift_right_logical(codes, 9)
        col_of = jnp.bitwise_and(codes, 511)
        right = jnp.concatenate(
            [jnp.where(here == col_of[s : s + 1], 1.0, 0.0).astype(BF16) for s in range(8)], axis=1
        )
        total = jnp.zeros((B, B), F32)
        for part in parts:
            left = jnp.concatenate(
                [jnp.where(here == row_of[s : s + 1], part[s : s + 1], 0.0).astype(BF16) for s in range(8)],
                axis=1,
            )
            total = total + dot_nt(left, right)
        out_ref[slot] = out_ref[slot] - total
        return carry

    lax.fori_loop(0, lax.div(steps + 7, 8), scatter, 0)

    @pl.when(c == lax.rem(r, 8))
    def _():
        own = jnp.where(mine, flux, 0.0)
        parts = pieces(own)
        high = lax.shift_right_logical(low_row, 7)
        low = jnp.bitwise_and(low_row, 127)
        here8 = lax.broadcasted_iota(jnp.int32, (8, LANES), 0)
        here128 = lax.broadcasted_iota(jnp.int32, (LANES, LANES), 0)
        total = jnp.zeros((24, LANES), F32)
        for g in range(ROWS // 8):
            ones = []
            lefts = []
            for s in range(8 * g, 8 * g + 8):
                ones.append(jnp.where(here128 == low[s : s + 1], 1.0, 0.0).astype(BF16))
                at = here8 == high[s : s + 1]
                lefts.append(
                    jnp.concatenate([jnp.where(at, part[s : s + 1], 0.0) for part in parts], axis=0).astype(BF16)
                )
            total = total + dot_nt(jnp.concatenate(lefts, axis=1), jnp.concatenate(ones, axis=1))
        diagonal = total[0:8] + total[8:16] + total[16:24]
        eye = here128 == lax.broadcasted_iota(jnp.int32, (LANES, LANES), 1)
        which = jnp.where(upper, 0, 1)
        for t in range(4):
            part = pl.ds(t * LANES, LANES)
            out_ref[which, part, part] = out_ref[which, part, part] + jnp.where(eye, diagonal[t : t + 1], 0.0)


def add_weirs(base, block_mask, every_head, coef, weir_node, weir_cell):
    pad = ROWS * LANES - coef.shape[0]
    coef = jnp.pad(coef, (0, pad)).reshape(ROWS, LANES)
    node = jnp.pad(weir_node, (0, pad)).reshape(ROWS, LANES)
    cell = jnp.pad(weir_cell, (0, pad), constant_values=4096).reshape(ROWS, LANES)
    vmem = pl.BlockSpec(memory_space=pltpu.VMEM)
    return pl.pallas_call(
        weirs_kernel,
        out_shape=jax.ShapeDtypeStruct((2, B, B), F32),
        in_specs=[pl.BlockSpec(memory_space=pltpu.SMEM)] + [vmem] * 5,
        out_specs=vmem,
        scratch_shapes=[pltpu.VMEM((ROWS, LANES), jnp.int32), pltpu.VMEM((ROWS, LANES), F32)],
        compiler_params=pltpu.CompilerParams(vmem_limit_bytes=VMEM_LIMIT),
        name="add_weirs",
    )(block_mask, base, every_head, coef, node, cell)


def eliminate_kernel(
    a_ref, out_ref, side, panel, pivot, ph, pl_, sh, sl, xf, wide_send, wide_recv, pair_recv, side_send, side_recv
):
    r = lax.axis_index("wide")
    c = lax.axis_index("narrow")
    core = lax.rem(r, 2)
    y = lax.rem(lax.div(r, 2), 4)
    x = lax.div(r, 8)
    z = lax.rem(c, 4)
    far = lax.div(c, 4)
    up = (x * 8 + lax.rem(y + 1, 4) * 2 + core, c)
    down = (x * 8 + lax.rem(y + 3, 4) * 2 + core, c)
    across = ((1 - x) * 8 + y * 2 + core, c)
    pair = (x * 8 + y * 2 + 1 - core, c)
    ahead = (r, far * 4 + lax.rem(z + 1, 4))
    behind = (r, far * 4 + lax.rem(z + 3, 4))
    over = (r, (1 - far) * 4 + z)
    near_x = x == 0

    barrier = pltpu.get_barrier_semaphore()
    for peer in (up, down, across, pair, ahead, behind, over):
        pl.semaphore_signal(barrier, inc=1, device_id=peer, device_id_type=MESH)
    pl.semaphore_wait(barrier, 7)

    def either(*terms):
        out = terms[0]
        for term in terms[1:]:
            out = out | term
        return out

    far_x = x == 1
    tree_up = (either(near_x & (y < 3), far_x & (y == 2)), far_x & (y == 3), far_x & (y < 2))
    tree_down = (far_x & (y == 1), either(near_x & (y != 1), far_x & (y >= 2)), far_x & (y == 0))
    tree_across = (
        near_x & ((y == 1) | (y == 2)),
        near_x & (y == 3),
        either(near_x & (y == 0), far_x & (y > 0)),
    )

    def wide_chunk(half, tree):
        start, size = TREE_ROWS[tree]
        return panel.at[core, lax.div(half, 2), pl.ds(pl.multiple_of(lax.rem(half, 2) * 256 + start, 8), size)]

    def wide_copy(half, tree, way, target):
        chunk = wide_chunk(half, tree)
        at = half * 3 + tree
        return pltpu.make_async_remote_copy(
            src_ref=chunk,
            dst_ref=chunk,
            send_sem=wide_send.at[at, way],
            recv_sem=(pair_recv if way == 3 else wide_recv).at[at],
            device_id=target,
            device_id_type=MESH,
        )

    def each_way(half, tree, act):
        for way, (target, when) in enumerate(
            ((up, tree_up[tree]), (down, tree_down[tree]), (across, tree_across[tree]))
        ):

            @pl.when(when)
            def _():
                act(wide_copy(half, tree, way, target))

        act(wide_copy(half, tree, 3, pair))

    def wide_start(half):
        for tree in range(3):
            each_way(half, tree, lambda copy: copy.start())

    def wide_relay(half):
        for tree in range(3):
            wide_copy(half, tree, 0, up).wait_recv()
            each_way(half, tree, lambda copy: copy.start())

    def pair_wait(first, last):
        def one(half, carry):
            for tree in range(3):
                start, size = TREE_ROWS[tree]
                rows = pl.ds(pl.multiple_of(lax.rem(half, 2) * 256 + start, 8), size)
                chunk = panel.at[1 - core, lax.div(half, 2), rows]
                pltpu.make_async_remote_copy(
                    src_ref=chunk,
                    dst_ref=chunk,
                    send_sem=wide_send.at[half * 3 + tree, 3],
                    recv_sem=pair_recv.at[half * 3 + tree],
                    device_id=pair,
                    device_id_type=MESH,
                ).wait_recv()
            return carry

        lax.fori_loop(first, last, one, 0)

    def side_copy(s, q, way, target):
        chunk = side.at[s, pl.ds(q * 128, 128)]
        return pltpu.make_async_remote_copy(
            src_ref=chunk,
            dst_ref=chunk,
            send_sem=side_send.at[s, q, way],
            recv_sem=side_recv.at[s, q],
            device_id=target,
            device_id_type=MESH,
        )

    near = far == 0
    away = far == 1

    def side_ways(s, q):
        rel = lax.rem(z + 4 - s, 4)
        if q < 2:
            ahead_near, behind_near = rel < 3, None
        else:
            ahead_near, behind_near = None, rel != 1
        if q % 2 == 0:
            ahead_far, behind_far = (rel == q) | (rel == (q + 1) % 4), rel == q
        else:
            ahead_far, behind_far = rel == q, (rel == q) | (rel == (q + 3) % 4)
        go_ahead = away & ahead_far if ahead_near is None else (near & ahead_near) | (away & ahead_far)
        go_behind = away & behind_far if behind_near is None else (near & behind_near) | (away & behind_far)
        return ((ahead, go_ahead), (behind, go_behind), (over, near & (rel == q)))

    def side_each(s, q, act):
        for way, (target, when) in enumerate(side_ways(s, q)):

            @pl.when(when)
            def _():
                act(side_copy(s, q, way, target))

    def side_relay(s, q):
        @pl.when(c != s)
        def _():
            side_copy(s, q, 0, ahead).wait_recv()

        side_each(s, q, lambda copy: copy.start())

    def side_source(s):
        @pl.when(c == s)
        def _():
            side[s] = a_ref[0]

    order = (1, 3, 0, 2)

    side_source(0)
    side_source(1)

    @pl.when(r < 2)
    def _():
        panel[core, 0] = a_ref[0]
        panel[core, 1] = a_ref[1]

    for q in order:
        side_relay(0, q)

    @pl.when(r < 2)
    def _():
        for half in range(4):
            wide_start(half)

    @pl.when(r >= 2)
    def _():
        lax.fori_loop(0, 4, lambda half, carry: (wide_relay(half), carry)[1], 0)

    for q in order:
        side_relay(1, q)

    @pl.when(r == 0)
    def _():
        panel[0, 2] = side[1]

    @pl.when(r == 1)
    def _():
        panel[1, 2] = side[0]

    @pl.when(r < 2)
    def _():
        for half in (4, 5):
            wide_start(half)

    @pl.when(r >= 2)
    def _():
        lax.fori_loop(4, 6, lambda half, carry: (wide_relay(half), carry)[1], 0)

    def put(index, value):
        high, low = split(value)
        ph[index] = high
        pl_[index] = low

    def times(i, j):
        return product(ph[i], pl_[i], ph[j], pl_[j])

    @pl.when(r == 0)
    def _():
        pivot[...] = side[0]

    @pl.when(r >= 1)
    def _():
        @pl.when(core == 0)
        def _():
            lax.fori_loop(6, 8, lambda half, carry: (wide_relay(half), carry)[1], 0)

        @pl.when(core == 1)
        def _():
            pair_wait(0, 8)

        put(0, panel[0, 3])
        put(1, panel[0, 2])
        put(2, times(0, 1))
        put(3, side[0])
        reduced = side[1] - times(3, 2)
        pivot[...] = reduced
        put(4, reduced)

    @pl.when(r < 2)
    def _():
        here = lax.broadcasted_iota(jnp.int32, (B, B), 0) == lax.broadcasted_iota(jnp.int32, (B, B), 1)
        block = pivot[...]
        only = jnp.where(here, block, 0.0)
        one_row = 1.0 / jnp.sum(only, axis=0, keepdims=True)
        one_col = 1.0 / jnp.sum(only, axis=1, keepdims=True)
        eye = jnp.where(here, 1.0, 0.0)
        rest = eye - block * one_row
        xf[...] = one_col * (eye + rest)
        high, low = split(rest)
        sh[0, B:] = high
        sl[0, B:] = low
        high, low = split(product(sh[0, B:], sl[0, B:], sh[0, B:], sl[0, B:]))
        sh[1, B:] = high
        sl[1, B:] = low
        high, low = split(xf[...])
        sh[1, :B] = high
        sl[1, :B] = low

        def step(k, carry):
            now = lax.rem(k, 2)
            later = 1 - now
            both = product(sh[now], sl[now], sh[now, B:], sl[now, B:])
            total = xf[...] + both[:B]
            xf[...] = total
            high, low = split(total)
            sh[later, :B] = high
            sl[later, :B] = low
            high, low = split(both[B:])
            sh[later, B:] = high
            sl[later, B:] = low
            return carry

        lax.fori_loop(1, NS_STEPS - 1, step, 0)
        now = (NS_STEPS - 1) % 2
        panel[core, 3] = xf[...] + product(sh[now, :B], sl[now, :B], sh[now, B:], sl[now, B:])
        for half in (6, 7):
            wide_start(half)

    @pl.when(r == 0)
    def _():
        put(0, panel[0, 3])
        for j in range(2):
            put(1, a_ref[j])
            out_ref[j] = times(0, 1)
        pair_wait(0, 8)

    @pl.when(r >= 1)
    def _():
        for j in range(2):
            put(1, panel[0, j])
            put(5 + j, times(0, 1))
            kept = a_ref[j] - times(3, 5 + j)
            out_ref[j] = kept

            @pl.when(r == 1)
            def _():
                put(7 + j, kept)

        @pl.when(r >= 2)
        def _():
            @pl.when(core == 0)
            def _():
                pair_wait(0, 6)

            put(1, panel[1, 2])
            for j in range(2):
                put(7 + j, panel[1, j] - times(1, 5 + j))

            @pl.when(core == 1)
            def _():
                lax.fori_loop(6, 8, lambda half, carry: (wide_relay(half), carry)[1], 0)

            @pl.when(core == 0)
            def _():
                pair_wait(6, 8)

        put(0, panel[1, 3])
        for j in range(2):
            scaled = times(0, 7 + j)
            live = c >= 2 if j == 0 else c >= 0

            @pl.when((r == 1) & live)
            def _():
                out_ref[j] = scaled

            @pl.when((r >= 2) & live)
            def _():
                put(5, scaled)
                out_ref[j] = out_ref[j] - times(4, 5)

    @pl.when(c == 0)
    def _():
        out_ref[0] = a_ref[0]

    def sent(half, carry):
        for tree in range(3):
            each_way(half, tree, lambda copy: copy.wait_send())
        return carry

    lax.fori_loop(0, 8, sent, 0)
    for s in range(2):
        for q in range(4):
            side_each(s, q, lambda copy: copy.wait_send())


def eliminate(blocks):
    vmem = pl.BlockSpec(memory_space=pltpu.VMEM)
    dma = pltpu.SemaphoreType.DMA
    return pl.pallas_call(
        eliminate_kernel,
        out_shape=jax.ShapeDtypeStruct((2, B, B), F32),
        in_specs=[vmem],
        out_specs=vmem,
        scratch_shapes=[
            pltpu.VMEM((2, B, B), F32),
            pltpu.VMEM((2, 4, B, B), F32),
            pltpu.VMEM((B, B), F32),
            pltpu.VMEM((9, B, B), BF16),
            pltpu.VMEM((9, B, B), BF16),
            pltpu.VMEM((2, 2 * B, B), BF16),
            pltpu.VMEM((2, 2 * B, B), BF16),
            pltpu.VMEM((B, B), F32),
            dma((24, 4)),
            dma((24,)),
            dma((24,)),
            dma((2, 4, 3)),
            dma((2, 4)),
        ],
        compiler_params=pltpu.CompilerParams(
            collective_id=1, has_side_effects=True, vmem_limit_bytes=VMEM_LIMIT
        ),
        name="eliminate",
    )(blocks)


def per_device(base, block_mask, heads, coef, weir_node, weir_cell):
    blocks = base.reshape(2, B, B)
    every_head = gather_heads(heads)
    blocks = add_weirs(blocks, block_mask, every_head, coef, weir_node, weir_cell)
    return eliminate(blocks).reshape(base.shape)


def solution(mesh):
    placed = (P(None, "wide", None, "narrow", None, None), P(), P("narrow"), P(), P(), P())
    return jax.shard_map(
        per_device,
        mesh=mesh,
        in_specs=placed,
        out_specs=P(None, "wide", None, "narrow", None, None),
        check_vma=False,
    )
```

time: 884 us -> 433 us (0.49)
  waiting for transfers between devices: 473 us -> 0 us
  Pallas kernels: 0 us -> 422 us
  other arithmetic: 203 us -> 0 us
  local copies, waits for them, and re-layouts: 115 us -> 5.89 us
  matrix products: 28 us -> 0 us
  blocking collectives: 27.7 us -> 0 us
  between operations: 13.9 us -> 0.02 us
  loops' own time: 11.5 us -> 0 us
    psum x4 -> x0, waiting for transfers between devices: 473 us -> none  [spread(): return lax.psum(jnp.where(mine, shard, jnp.zeros_like(shard)), axis)]
    pallas_call x0 -> x3, Pallas kernels: none -> 422 us  [the longest x1 405 us: eliminate(): pl.pallas_call(eliminate_kernel, out_shape=jax.ShapeDtypeStruct((2, B, B)...]
    unnamed x6 -> x0, other arithmetic: 192 us -> none
    gather x3 -> x0, local copies, waits for them, and re-layouts: 94.1 us -> none  [the longest x2 93.4 us: per_device(): drop = every_head[weir_node] - every_head[weir_cell]]
    dot_general x4 -> x0, matrix products: 28 us -> none  [the longest x2 16.5 us: panel(): jnp.einsum('pq,jqs->jps', inverse, blocks[local_row], precision=lax.Preci...]
    all_gather x1 -> x0, blocking collectives: 27.7 us -> none  [per_device(): every_head = lax.all_gather(heads, 'narrow', axis=0, tiled=True)]
    another operation x2 -> x0, loops' own time: 11.5 us -> none  [panel(): lax.cond(owner, newton_schulz, jnp.zeros_like, blocks[local_row, local_col])]
  transfers between devices with their start and end apart: 4 -> 0, of which waited for: 4 -> 0; matrix products, arithmetic and copies ran while one was open for 1% -> 0% of each run, Pallas kernels for 0% -> 0%
where the time goes in v1:
time: 433 us; the launch traced here: 428 us
  Pallas kernels  422 us (97%)
  local copies, waits for them, and re-layouts  5.89 us (1%)
    pallas_call x1, Pallas kernels, eliminate(): pl.pallas_call(eliminate_kernel, out_shape=jax.ShapeDtypeStruct((2, B, B)...  405 us
    pallas_call x1, Pallas kernels, gather_heads(): pl.pallas_call(gather_heads_kernel, out_shape=jax.ShapeDtypeStruct((64, L...  9.79 us

profile of v1, /device:TPU:21, one launch (start us, length us, event | category | flops | bytes accessed | tf_op | source)
XLA Modules:
  0.0 427.6 jit_solution(13338993371481534720)
XLA Ops:
  0.0 9.8 %gather_heads.1.heads_ref = f32[64,128]{1,0:T(8,128)} custom-call(f32[8,128]{1,0:T(8,128)} %bitcast.13), custom_call_target="tpu_custom_call" | custom-call | tf_op jit(solution)/shard_map/gather_heads/pallas_call | solution.py:65
  9.8 1.4 pad_bitcast_fusion.2.coef_ref
  11.2 1.4 pad_bitcast_fusion
  12.6 6.7 %add_weirs.1.a_ref = f32[2,512,512]{2,1,0:T(8,128)} custom-call(s32[16,16]{1,0:T(8,128)} %mask_ref.1, f32[2,512,512]{2,1,0:T(8,128)} %bitcast.12, f32[64,128]{1,0:T(8,128)} %gather_heads.1.heads_ref, f32[72,128]{1,0:T(8,128)} %pad_bitcast_fusion.2.coef_ref, s32[72,128]{1,0:T(8,128)} %get-tuple-element.6.node_ref, s32[72,128]{1,0:T(8,128)} %get-tuple-element.5.cell_ref), custom_call_target="tpu_custom_call" | custom-call | tf_op jit(solution)/shard_map/add_weirs/pallas_call | solution.py:184
  19.3 405.2 %eliminate.1 = f32[2,512,512]{2,1,0:T(8,128)} custom-call(f32[2,512,512]{2,1,0:T(8,128)} %add_weirs.1.a_ref), custom_call_target="tpu_custom_call" | custom-call | tf_op jit(solution)/shard_map/eliminate/pallas_call | solution.py:517
  424.5 3.1 copy.9

commit v2 on v1

--- a/solution.py
+++ b/solution.py
@@ -15,7 +15,6 @@
 F32 = jnp.float32
 BF16 = jnp.bfloat16
 VMEM_LIMIT = 56 * 2**20
-TREE_ROWS = ((0, 88), (88, 88), (176, 80))
 
 
 def split(x):
@@ -193,186 +192,141 @@
 
 
 def eliminate_kernel(
-    a_ref, out_ref, side, panel, pivot, ph, pl_, sh, sl, xf, wide_send, wide_recv, pair_recv, side_send, side_recv
+    a_ref,
+    out_ref,
+    side,
+    row,
+    extra,
+    pivot,
+    ph,
+    pl_,
+    sh,
+    sl,
+    xf,
+    side_send,
+    side_recv,
+    row_send,
+    row_recv,
+    extra_send,
+    extra_recv,
+    turn,
 ):
     r = lax.axis_index("wide")
     c = lax.axis_index("narrow")
     core = lax.rem(r, 2)
-    y = lax.rem(lax.div(r, 2), 4)
-    x = lax.div(r, 8)
-    z = lax.rem(c, 4)
-    far = lax.div(c, 4)
-    up = (x * 8 + lax.rem(y + 1, 4) * 2 + core, c)
-    down = (x * 8 + lax.rem(y + 3, 4) * 2 + core, c)
-    across = ((1 - x) * 8 + y * 2 + core, c)
-    pair = (x * 8 + y * 2 + 1 - core, c)
-    ahead = (r, far * 4 + lax.rem(z + 1, 4))
-    behind = (r, far * 4 + lax.rem(z + 3, 4))
-    over = (r, (1 - far) * 4 + z)
-    near_x = x == 0
+    chip = lax.div(r, 2)
+    pair = (chip * 2 + 1 - core, c)
 
     barrier = pltpu.get_barrier_semaphore()
-    for peer in (up, down, across, pair, ahead, behind, over):
-        pl.semaphore_signal(barrier, inc=1, device_id=peer, device_id_type=MESH)
-    pl.semaphore_wait(barrier, 7)
-
-    def either(*terms):
-        out = terms[0]
-        for term in terms[1:]:
-            out = out | term
-        return out
-
-    far_x = x == 1
-    tree_up = (either(near_x & (y < 3), far_x & (y == 2)), far_x & (y == 3), far_x & (y < 2))
-    tree_down = (far_x & (y == 1), either(near_x & (y != 1), far_x & (y >= 2)), far_x & (y == 0))
-    tree_across = (
-        near_x & ((y == 1) | (y == 2)),
-        near_x & (y == 3),
-        either(near_x & (y == 0), far_x & (y > 0)),
-    )
-
-    def wide_chunk(half, tree):
-        start, size = TREE_ROWS[tree]
-        return panel.at[core, lax.div(half, 2), pl.ds(pl.multiple_of(lax.rem(half, 2) * 256 + start, 8), size)]
-
-    def wide_copy(half, tree, way, target):
-        chunk = wide_chunk(half, tree)
-        at = half * 3 + tree
+    for hop in range(1, 16):
+        pl.semaphore_signal(barrier, inc=1, device_id=(lax.rem(r + hop, 16), c), device_id_type=MESH)
+    for hop in range(1, 8):
+        pl.semaphore_signal(barrier, inc=1, device_id=(r, lax.rem(c + hop, 8)), device_id_type=MESH)
+    pl.semaphore_wait(barrier, 22)
+
+    def loop(first, last, act):
+        lax.fori_loop(first, last, lambda i, carry: (act(i), carry)[1], 0)
+
+    def side_copy(s, piece, at, target):
+        chunk = side.at[s, pl.ds(pl.multiple_of(piece * 64, 64), 64)]
         return pltpu.make_async_remote_copy(
             src_ref=chunk,
             dst_ref=chunk,
-            send_sem=wide_send.at[at, way],
-            recv_sem=(pair_recv if way == 3 else wide_recv).at[at],
-            device_id=target,
+            send_sem=side_send.at[s, at],
+            recv_sem=side_recv.at[s, piece],
+            device_id=(r, target),
             device_id_type=MESH,
         )
 
-    def each_way(half, tree, act):
-        for way, (target, when) in enumerate(
-            ((up, tree_up[tree]), (down, tree_down[tree]), (across, tree_across[tree]))
-        ):
-
-            @pl.when(when)
+    def side_source(s, act):
+        def one(hop):
+            target = lax.rem(c + hop, 8)
+            act(side_copy(s, target, hop, target))
+            act(side_copy(s, c, 8 + hop, target))
+
+        @pl.when(c == s)
+        def _():
+            loop(1, 8, one)
+
+    def side_relay(s, act, wait):
+        def one(hop):
+            target = lax.rem(c + hop, 8)
+
+            @pl.when(target != s)
             def _():
-                act(wide_copy(half, tree, way, target))
-
-        act(wide_copy(half, tree, 3, pair))
-
-    def wide_start(half):
-        for tree in range(3):
-            each_way(half, tree, lambda copy: copy.start())
-
-    def wide_relay(half):
-        for tree in range(3):
-            wide_copy(half, tree, 0, up).wait_recv()
-            each_way(half, tree, lambda copy: copy.start())
-
-    def pair_wait(first, last):
-        def one(half, carry):
-            for tree in range(3):
-                start, size = TREE_ROWS[tree]
-                rows = pl.ds(pl.multiple_of(lax.rem(half, 2) * 256 + start, 8), size)
-                chunk = panel.at[1 - core, lax.div(half, 2), rows]
-                pltpu.make_async_remote_copy(
-                    src_ref=chunk,
-                    dst_ref=chunk,
-                    send_sem=wide_send.at[half * 3 + tree, 3],
-                    recv_sem=pair_recv.at[half * 3 + tree],
-                    device_id=pair,
-                    device_id_type=MESH,
-                ).wait_recv()
-            return carry
-
-        lax.fori_loop(first, last, one, 0)
-
-    def side_copy(s, q, way, target):
-        chunk = side.at[s, pl.ds(q * 128, 128)]
+                act(side_copy(s, c, hop, target))
+
+        @pl.when(c != s)
+        def _():
+            if wait:
+                side_copy(s, c, 0, c).wait_recv()
+            loop(1, 8, one)
+
+    def side_wait(s):
+        def one(hop):
+            piece = lax.rem(c + hop, 8)
+            side_copy(s, piece, 0, c).wait_recv()
+
+        @pl.when(c != s)
+        def _():
+            loop(1, 8, one)
+
+    def row_copy(b, piece, at, target):
+        chunk = row.at[b, pl.ds(pl.multiple_of(piece * 32, 32), 32)]
         return pltpu.make_async_remote_copy(
             src_ref=chunk,
             dst_ref=chunk,
-            send_sem=side_send.at[s, q, way],
-            recv_sem=side_recv.at[s, q],
-            device_id=target,
+            send_sem=row_send.at[b, at],
+            recv_sem=row_recv.at[b, piece],
+            device_id=(target, c),
             device_id_type=MESH,
         )
 
-    near = far == 0
-    away = far == 1
-
-    def side_ways(s, q):
-        rel = lax.rem(z + 4 - s, 4)
-        if q < 2:
-            ahead_near, behind_near = rel < 3, None
-        else:
-            ahead_near, behind_near = None, rel != 1
-        if q % 2 == 0:
-            ahead_far, behind_far = (rel == q) | (rel == (q + 1) % 4), rel == q
-        else:
-            ahead_far, behind_far = rel == q, (rel == q) | (rel == (q + 3) % 4)
-        go_ahead = away & ahead_far if ahead_near is None else (near & ahead_near) | (away & ahead_far)
-        go_behind = away & behind_far if behind_near is None else (near & behind_near) | (away & behind_far)
-        return ((ahead, go_ahead), (behind, go_behind), (over, near & (rel == q)))
-
-    def side_each(s, q, act):
-        for way, (target, when) in enumerate(side_ways(s, q)):
-
-            @pl.when(when)
+    def row_source(b, act):
+        def one(t):
+            act(row_copy(b, t, t, t))
+            act(row_copy(b, lax.rem(t, 2), 16 + t, t))
+
+        loop(2, 16, one)
+
+    def row_pass(b, act, wait):
+        def direct(hop):
+            target = lax.rem(chip + hop, 8)
+
+            @pl.when(target != 0)
             def _():
-                act(side_copy(s, q, way, target))
-
-    def side_relay(s, q):
-        @pl.when(c != s)
-        def _():
-            side_copy(s, q, 0, ahead).wait_recv()
-
-        side_each(s, q, lambda copy: copy.start())
-
-    def side_source(s):
-        @pl.when(c == s)
-        def _():
-            side[s] = a_ref[0]
-
-    order = (1, 3, 0, 2)
-
-    side_source(0)
-    side_source(1)
-
-    @pl.when(r < 2)
-    def _():
-        panel[core, 0] = a_ref[0]
-        panel[core, 1] = a_ref[1]
-
-    for q in order:
-        side_relay(0, q)
-
-    @pl.when(r < 2)
-    def _():
-        for half in range(4):
-            wide_start(half)
-
-    @pl.when(r >= 2)
-    def _():
-        lax.fori_loop(0, 4, lambda half, carry: (wide_relay(half), carry)[1], 0)
-
-    for q in order:
-        side_relay(1, q)
-
-    @pl.when(r == 0)
-    def _():
-        panel[0, 2] = side[1]
-
-    @pl.when(r == 1)
-    def _():
-        panel[1, 2] = side[0]
-
-    @pl.when(r < 2)
-    def _():
-        for half in (4, 5):
-            wide_start(half)
-
-    @pl.when(r >= 2)
-    def _():
-        lax.fori_loop(4, 6, lambda half, carry: (wide_relay(half), carry)[1], 0)
+                act(row_copy(b, r, hop, target * 2 + core))
+
+        def over(hop):
+            piece = lax.rem(chip + hop, 8) * 2 + core
+            if wait:
+                row_copy(b, piece, 0, r).wait_recv()
+            act(row_copy(b, piece, 8 + hop, pair[0]))
+
+        if wait:
+            row_copy(b, r, 0, r).wait_recv()
+        loop(1, 8, direct)
+        act(row_copy(b, r, 8, pair[0]))
+        loop(1, 8, over)
+
+    def row_wait(b):
+        def one(q):
+            row_copy(b, q * 2 + 1 - core, 0, r).wait_recv()
+
+        loop(0, 8, one)
+
+    def extra_copy(src, at):
+        return pltpu.make_async_remote_copy(
+            src_ref=src,
+            dst_ref=extra.at[at],
+            send_sem=extra_send.at[at],
+            recv_sem=extra_recv.at[at],
+            device_id=pair,
+            device_id_type=MESH,
+        )
+
+    start = lambda copy: copy.start()
+    sent = lambda copy: copy.wait_send()
 
     def put(index, value):
         high, low = split(value)
@@ -382,30 +336,7 @@
     def times(i, j):
         return product(ph[i], pl_[i], ph[j], pl_[j])
 
-    @pl.when(r == 0)
-    def _():
-        pivot[...] = side[0]
-
-    @pl.when(r >= 1)
-    def _():
-        @pl.when(core == 0)
-        def _():
-            lax.fori_loop(6, 8, lambda half, carry: (wide_relay(half), carry)[1], 0)
-
-        @pl.when(core == 1)
-        def _():
-            pair_wait(0, 8)
-
-        put(0, panel[0, 3])
-        put(1, panel[0, 2])
-        put(2, times(0, 1))
-        put(3, side[0])
-        reduced = side[1] - times(3, 2)
-        pivot[...] = reduced
-        put(4, reduced)
-
-    @pl.when(r < 2)
-    def _():
+    def invert():
         here = lax.broadcasted_iota(jnp.int32, (B, B), 0) == lax.broadcasted_iota(jnp.int32, (B, B), 1)
         block = pivot[...]
         only = jnp.where(here, block, 0.0)
@@ -424,7 +355,7 @@
         sh[1, :B] = high
         sl[1, :B] = low
 
-        def step(k, carry):
+        def step(k):
             now = lax.rem(k, 2)
             later = 1 - now
             both = product(sh[now], sl[now], sh[now, B:], sl[now, B:])
@@ -436,55 +367,127 @@
             high, low = split(both[B:])
             sh[later, B:] = high
             sl[later, B:] = low
-            return carry
-
-        lax.fori_loop(1, NS_STEPS - 1, step, 0)
+
+        loop(1, NS_STEPS - 1, step)
         now = (NS_STEPS - 1) % 2
-        panel[core, 3] = xf[...] + product(sh[now, :B], sl[now, :B], sh[now, B:], sl[now, B:])
-        for half in (6, 7):
-            wide_start(half)
+        return xf[...] + product(sh[now, :B], sl[now, :B], sh[now, B:], sl[now, B:])
+
+    @pl.when(c == 0)
+    def _():
+        side[0] = a_ref[0]
+
+    @pl.when((c == 1) & (r < 2))
+    def _():
+        side[1] = a_ref[0]
+
+    @pl.when(r == 1)
+    def _():
+        pl.semaphore_wait(turn, 1)
+
+    side_source(0, start)
+    side_relay(0, start, True)
+    side_wait(0)
 
     @pl.when(r == 0)
     def _():
-        put(0, panel[0, 3])
+        pl.semaphore_signal(turn, inc=1, device_id=pair, device_id_type=MESH)
+
+    @pl.when(r < 2)
+    def _():
+        side_source(1, start)
+
+    @pl.when(r == 0)
+    def _():
+        extra_copy(a_ref.at[0], 1).start()
+        extra_copy(a_ref.at[1], 2).start()
+        pivot[...] = side[0]
+        xf_first = invert()
+        xf[...] = xf_first
+        extra_copy(xf, 0).start()
+        put(0, xf_first)
+        side_relay(1, start, True)
+        side_wait(1)
+        put(1, side[1])
+        put(2, times(0, 1))
+        for at in (0, 1):
+            extra_copy(extra.at[at], at).wait_recv()
+        put(3, extra[0])
+        pivot[...] = extra[1] - times(3, 2)
+        extra_copy(xf, 0).wait_send()
+        row[4] = invert()
+        row_source(4, start)
+        extra_copy(row.at[4], 3).start()
         for j in range(2):
             put(1, a_ref[j])
             out_ref[j] = times(0, 1)
-        pair_wait(0, 8)
+        row_source(4, sent)
+        for at in (1, 2):
+            extra_copy(a_ref.at[at - 1], at).wait_send()
+
+    @pl.when(r == 1)
+    def _():
+        extra_copy(side.at[0], 0).start()
+        side_relay(1, start, True)
+        side_wait(1)
+        extra_copy(side.at[1], 1).start()
+        for at in range(3):
+            extra_copy(extra.at[at], at).wait_recv()
+        put(0, extra[0])
+        put(3, side[0])
+        for j in range(2):
+            put(1, extra[1 + j])
+            scaled = times(0, 1)
+            row[j] = scaled
+            row_source(j, start)
+            put(4 + j, scaled)
+        for j in range(2):
+            kept = a_ref[j] - times(3, 4 + j)
+            row[2 + j] = kept
+            row_source(2 + j, start)
+            out_ref[j] = kept
+            put(6 + j, kept)
+
+    @pl.when(r >= 2)
+    def _():
+        put(3, side[0])
+        for j in range(2):
+            row_pass(j, start, True)
+        for j in range(2):
+            row_wait(j)
+            put(4 + j, row[j])
+            kept = a_ref[j] - times(3, 4 + j)
+            out_ref[j] = kept
+            if j == 0:
+
+                @pl.when(c == 1)
+                def _():
+                    side[1] = kept
+
+                side_source(1, start)
+        for j in range(2):
+            row_pass(2 + j, start, True)
+        side_relay(1, start, True)
+        for j in range(2):
+            row_wait(2 + j)
+            put(6 + j, row[2 + j])
+        side_wait(1)
+        put(4, side[1])
+        row_pass(4, start, True)
+        row_wait(4)
+
+    @pl.when(r == 1)
+    def _():
+        extra_copy(row.at[4], 3).wait_recv()
+        put(0, extra[3])
+
+    @pl.when(r >= 2)
+    def _():
+        put(0, row[4])
 
     @pl.when(r >= 1)
     def _():
         for j in range(2):
-            put(1, panel[0, j])
-            put(5 + j, times(0, 1))
-            kept = a_ref[j] - times(3, 5 + j)
-            out_ref[j] = kept
-
-            @pl.when(r == 1)
-            def _():
-                put(7 + j, kept)
-
-        @pl.when(r >= 2)
-        def _():
-            @pl.when(core == 0)
-            def _():
-                pair_wait(0, 6)
-
-            put(1, panel[1, 2])
-            for j in range(2):
-                put(7 + j, panel[1, j] - times(1, 5 + j))
-
-            @pl.when(core == 1)
-            def _():
-                lax.fori_loop(6, 8, lambda half, carry: (wide_relay(half), carry)[1], 0)
-
-            @pl.when(core == 0)
-            def _():
-                pair_wait(6, 8)
-
-        put(0, panel[1, 3])
-        for j in range(2):
-            scaled = times(0, 7 + j)
+            scaled = times(0, 6 + j)
             live = c >= 2 if j == 0 else c >= 0
 
             @pl.when((r == 1) & live)
@@ -500,15 +503,24 @@
     def _():
         out_ref[0] = a_ref[0]
 
-    def sent(half, carry):
-        for tree in range(3):
-            each_way(half, tree, lambda copy: copy.wait_send())
-        return carry
-
-    lax.fori_loop(0, 8, sent, 0)
     for s in range(2):
-        for q in range(4):
-            side_each(s, q, lambda copy: copy.wait_send())
+        side_source(s, sent)
+        side_relay(s, sent, False)
+
+    @pl.when(r == 0)
+    def _():
+        extra_copy(row.at[4], 3).wait_send()
+
+    @pl.when(r == 1)
+    def _():
+        for at in (0, 1):
+            extra_copy(side.at[at], at).wait_send()
+        for b in range(4):
+            row_source(b, sent)
+
+    @pl.when(r >= 2)
+    def _():
+        loop(0, 5, lambda b: row_pass(b, sent, False))
 
 
 def eliminate(blocks):
@@ -521,18 +533,21 @@
         out_specs=vmem,
         scratch_shapes=[
             pltpu.VMEM((2, B, B), F32),
-            pltpu.VMEM((2, 4, B, B), F32),
+            pltpu.VMEM((5, B, B), F32),
+            pltpu.VMEM((4, B, B), F32),
             pltpu.VMEM((B, B), F32),
-            pltpu.VMEM((9, B, B), BF16),
-            pltpu.VMEM((9, B, B), BF16),
+            pltpu.VMEM((8, B, B), BF16),
+            pltpu.VMEM((8, B, B), BF16),
             pltpu.VMEM((2, 2 * B, B), BF16),
             pltpu.VMEM((2, 2 * B, B), BF16),
             pltpu.VMEM((B, B), F32),
-            dma((24, 4)),
-            dma((24,)),
-            dma((24,)),
-            dma((2, 4, 3)),
-            dma((2, 4)),
+            dma((2, 16)),
+            dma((2, 8)),
+            dma((5, 32)),
+            dma((5, 16)),
+            dma((4,)),
+            dma((4,)),
+            pltpu.SemaphoreType.REGULAR,
         ],
         compiler_params=pltpu.CompilerParams(
             collective_id=1, has_side_effects=True, vmem_limit_bytes=VMEM_LIMIT

time: 433 us -> 198 us (0.46)
  Pallas kernels: 422 us -> 189 us
    pallas_call x1, Pallas kernels: 405 us -> 172 us  [eliminate(): pl.pallas_call(eliminate_kernel, out_shape=jax.ShapeDtypeStruct((2, B, B)...]
where the time goes in v2:
time: 198 us; the launch traced here: 195 us
  Pallas kernels  189 us (95%)
  local copies, waits for them, and re-layouts  5.89 us (3%)
    pallas_call x1, Pallas kernels, eliminate(): pl.pallas_call(eliminate_kernel, out_shape=jax.ShapeDtypeStruct((2, B, B)...  172 us
    pallas_call x1, Pallas kernels, gather_heads(): pl.pallas_call(gather_heads_kernel, out_shape=jax.ShapeDtypeStruct((64, L...  9.79 us
    pallas_call x1, Pallas kernels, add_weirs(): pl.pallas_call(weirs_kernel, out_shape=jax.ShapeDtypeStruct((2, B, B), F3...  6.6 us

profile of v2, /device:TPU:21, one launch (start us, length us, event | category | flops | bytes accessed | tf_op | source)
XLA Modules:
  0.0 194.5 jit_solution(7145545180404061172)
XLA Ops:
  0.0 9.8 %gather_heads.1.heads_ref = f32[64,128]{1,0:T(8,128)} custom-call(f32[8,128]{1,0:T(8,128)} %bitcast.13), custom_call_target="tpu_custom_call" | custom-call | tf_op jit(solution)/shard_map/gather_heads/pallas_call | solution.py:64
  9.8 1.4 pad_bitcast_fusion.2.coef_ref
  11.2 1.4 pad_bitcast_fusion
  12.6 6.6 %add_weirs.1.a_ref = f32[2,512,512]{2,1,0:T(8,128)} custom-call(s32[16,16]{1,0:T(8,128)} %mask_ref.1, f32[2,512,512]{2,1,0:T(8,128)} %bitcast.12, f32[64,128]{1,0:T(8,128)} %gather_heads.1.heads_ref, f32[72,128]{1,0:T(8,128)} %pad_bitcast_fusion.2.coef_ref, s32[72,128]{1,0:T(8,128)} %get-tuple-element.6.node_ref, s32[72,128]{1,0:T(8,128)} %get-tuple-element.5.cell_ref), custom_call_target="tpu_custom_call" | custom-call | tf_op jit(solution)/shard_map/add_weirs/pallas_call | solution.py:183
  19.2 172.2 %eliminate.1 = f32[2,512,512]{2,1,0:T(8,128)} custom-call(f32[2,512,512]{2,1,0:T(8,128)} %add_weirs.1.a_ref), custom_call_target="tpu_custom_call" | custom-call | tf_op jit(solution)/shard_map/eliminate/pallas_call | solution.py:529
  191.5 3.1 %copy.9 = f32[1,1,2,1,512,512]{5,4,3,2,1,0:T(8,128)} copy(f32[1,1,2,1,512,512]{5,4,3,2,1,0:T(8,128)} %bitcast.11) | data formatting | bytes 4194304

commit v3 on v1

--- a/solution.py
+++ b/solution.py
@@ -15,7 +15,20 @@
 F32 = jnp.float32
 BF16 = jnp.bfloat16
 VMEM_LIMIT = 56 * 2**20
-TREE_ROWS = ((0, 88), (88, 88), (176, 80))
+SLOTS = 2
+WIDE_DEPTH = ((0, 1, 2, 3, 3, 2, 3, 4), (0, 3, 2, 1, 3, 4, 3, 2), (0, 3, 4, 3, 1, 2, 3, 2))
+WIDE_WAYS = (
+    ((1, 1, 1, 0, 0, 0, 1, 0), (0, 0, 0, 0, 0, 1, 0, 0), (0, 1, 1, 0, 0, 0, 0, 0)),
+    ((0, 0, 0, 0, 0, 0, 0, 1), (1, 0, 1, 1, 0, 0, 1, 1), (0, 0, 0, 1, 0, 0, 0, 0)),
+    ((0, 0, 0, 0, 1, 1, 0, 0), (0, 0, 0, 0, 1, 0, 0, 0), (1, 0, 0, 0, 0, 1, 1, 1)),
+)
+SIDE_DEPTH = ((0, 1, 2, 3, 1, 2, 3, 2), (0, 1, 2, 3, 3, 2, 3, 4), (0, 3, 2, 1, 5, 4, 3, 4), (0, 3, 2, 1, 3, 4, 3, 2))
+SIDE_WAYS = (
+    ((1, 1, 1, 0, 1, 1, 0, 0), (0, 0, 0, 0, 1, 0, 0, 0), (1, 0, 0, 0, 0, 0, 0, 0)),
+    ((1, 1, 1, 0, 0, 1, 0, 0), (0, 0, 0, 0, 1, 1, 0, 0), (0, 1, 0, 0, 0, 0, 0, 0)),
+    ((0, 0, 0, 0, 0, 0, 1, 1), (1, 0, 1, 1, 0, 0, 1, 0), (0, 0, 1, 0, 0, 0, 0, 0)),
+    ((0, 0, 0, 0, 0, 0, 0, 1), (1, 0, 1, 1, 0, 0, 1, 1), (0, 0, 0, 1, 0, 0, 0, 0)),
+)
 
 
 def split(x):
@@ -193,186 +206,157 @@
 
 
 def eliminate_kernel(
-    a_ref, out_ref, side, panel, pivot, ph, pl_, sh, sl, xf, wide_send, wide_recv, pair_recv, side_send, side_recv
+    a_ref,
+    out_ref,
+    side,
+    panel,
+    last,
+    pivot,
+    ph,
+    pl_,
+    sh,
+    sl,
+    xf,
+    wide_send,
+    wide_recv,
+    pair_send,
+    pair_recv,
+    side_send,
+    side_recv,
+    last_sem,
 ):
     r = lax.axis_index("wide")
     c = lax.axis_index("narrow")
     core = lax.rem(r, 2)
-    y = lax.rem(lax.div(r, 2), 4)
-    x = lax.div(r, 8)
+    chip = lax.div(r, 2)
+    y = lax.rem(chip, 4)
+    x = lax.div(chip, 4)
     z = lax.rem(c, 4)
     far = lax.div(c, 4)
     up = (x * 8 + lax.rem(y + 1, 4) * 2 + core, c)
     down = (x * 8 + lax.rem(y + 3, 4) * 2 + core, c)
     across = ((1 - x) * 8 + y * 2 + core, c)
-    pair = (x * 8 + y * 2 + 1 - core, c)
+    pair = (chip * 2 + 1 - core, c)
     ahead = (r, far * 4 + lax.rem(z + 1, 4))
     behind = (r, far * 4 + lax.rem(z + 3, 4))
     over = (r, (1 - far) * 4 + z)
-    near_x = x == 0
 
     barrier = pltpu.get_barrier_semaphore()
     for peer in (up, down, across, pair, ahead, behind, over):
         pl.semaphore_signal(barrier, inc=1, device_id=peer, device_id_type=MESH)
     pl.semaphore_wait(barrier, 7)
 
-    def either(*terms):
-        out = terms[0]
-        for term in terms[1:]:
-            out = out | term
-        return out
-
-    far_x = x == 1
-    tree_up = (either(near_x & (y < 3), far_x & (y == 2)), far_x & (y == 3), far_x & (y < 2))
-    tree_down = (far_x & (y == 1), either(near_x & (y != 1), far_x & (y >= 2)), far_x & (y == 0))
-    tree_across = (
-        near_x & ((y == 1) | (y == 2)),
-        near_x & (y == 3),
-        either(near_x & (y == 0), far_x & (y > 0)),
-    )
-
-    def wide_chunk(half, tree):
-        start, size = TREE_ROWS[tree]
-        return panel.at[core, lax.div(half, 2), pl.ds(pl.multiple_of(lax.rem(half, 2) * 256 + start, 8), size)]
-
-    def wide_copy(half, tree, way, target):
-        chunk = wide_chunk(half, tree)
-        at = half * 3 + tree
+    def loop(first, last, act):
+        lax.fori_loop(first, last, lambda i, carry: (act(i), carry)[1], 0)
+
+    def pick(values, at):
+        return sum(jnp.where(at == i, v, 0) for i, v in enumerate(values) if v)
+
+    start = lambda copy: copy.start()
+    sent = lambda copy: copy.wait_send()
+
+    depth = tuple(pick(values, chip) for values in WIDE_DEPTH)
+    ways = tuple(tuple(pick(values, chip) == 1 for values in tree) for tree in WIDE_WAYS)
+
+    def wide_copy(j, way, target):
+        rows = pl.ds(pl.multiple_of(lax.rem(j, 8) * 64, 64), 64)
+        chunk = panel.at[core, lax.div(j, 8), rows]
         return pltpu.make_async_remote_copy(
             src_ref=chunk,
             dst_ref=chunk,
-            send_sem=wide_send.at[at, way],
-            recv_sem=(pair_recv if way == 3 else wide_recv).at[at],
+            send_sem=wide_send.at[j, way],
+            recv_sem=wide_recv.at[j],
             device_id=target,
             device_id_type=MESH,
         )
 
-    def each_way(half, tree, act):
-        for way, (target, when) in enumerate(
-            ((up, tree_up[tree]), (down, tree_down[tree]), (across, tree_across[tree]))
-        ):
-
-            @pl.when(when)
+    def wide_each(tree, j, act):
+        for way, target in enumerate((up, down, across)):
+
+            @pl.when(ways[tree][way])
             def _():
-                act(wide_copy(half, tree, way, target))
-
-        act(wide_copy(half, tree, 3, pair))
-
-    def wide_start(half):
+                act(wide_copy(j, way, target))
+
+    def wide_slot(first, end, slot):
         for tree in range(3):
-            each_way(half, tree, lambda copy: copy.start())
-
-    def wide_relay(half):
-        for tree in range(3):
-            wide_copy(half, tree, 0, up).wait_recv()
-            each_way(half, tree, lambda copy: copy.start())
-
-    def pair_wait(first, last):
-        def one(half, carry):
+            j = 3 * (slot - SLOTS * depth[tree]) + tree
+
+            @pl.when((j >= first) & (j < end))
+            def _():
+                wide_copy(j, 0, up).wait_recv()
+                wide_each(tree, j, start)
+
+    def wide_relay(first, end):
+        loop(first // 3 - 1, (end + 2) // 3 + 4 * SLOTS, lambda slot: wide_slot(first, end, slot))
+
+    def wide_source(first, end, act):
+        def one(j):
             for tree in range(3):
-                start, size = TREE_ROWS[tree]
-                rows = pl.ds(pl.multiple_of(lax.rem(half, 2) * 256 + start, 8), size)
-                chunk = panel.at[1 - core, lax.div(half, 2), rows]
-                pltpu.make_async_remote_copy(
-                    src_ref=chunk,
-                    dst_ref=chunk,
-                    send_sem=wide_send.at[half * 3 + tree, 3],
-                    recv_sem=pair_recv.at[half * 3 + tree],
-                    device_id=pair,
-                    device_id_type=MESH,
-                ).wait_recv()
-            return carry
-
-        lax.fori_loop(first, last, one, 0)
-
-    def side_copy(s, q, way, target):
-        chunk = side.at[s, pl.ds(q * 128, 128)]
+
+                @pl.when(lax.rem(j, 3) == tree)
+                def _():
+                    wide_each(tree, j, act)
+
+        loop(first, end, one)
+
+    def pair_copy(b):
+        block = panel.at[core, b]
+        return pltpu.make_async_remote_copy(
+            src_ref=block,
+            dst_ref=block,
+            send_sem=pair_send.at[b],
+            recv_sem=pair_recv.at[b],
+            device_id=pair,
+            device_id_type=MESH,
+        )
+
+    def pair_wait(b):
+        block = panel.at[1 - core, b]
+        pltpu.make_async_remote_copy(
+            src_ref=block,
+            dst_ref=block,
+            send_sem=pair_send.at[b],
+            recv_sem=pair_recv.at[b],
+            device_id=pair,
+            device_id_type=MESH,
+        ).wait_recv()
+
+    def side_copy(s, q, u, way, target):
+        chunk = side.at[s, pl.ds(pl.multiple_of(q * 128 + u * 64, 64), 64)]
         return pltpu.make_async_remote_copy(
             src_ref=chunk,
             dst_ref=chunk,
-            send_sem=side_send.at[s, q, way],
-            recv_sem=side_recv.at[s, q],
+            send_sem=side_send.at[s, q, u, way],
+            recv_sem=side_recv.at[s, q, u],
             device_id=target,
             device_id_type=MESH,
         )
 
-    near = far == 0
-    away = far == 1
-
-    def side_ways(s, q):
-        rel = lax.rem(z + 4 - s, 4)
-        if q < 2:
-            ahead_near, behind_near = rel < 3, None
-        else:
-            ahead_near, behind_near = None, rel != 1
-        if q % 2 == 0:
-            ahead_far, behind_far = (rel == q) | (rel == (q + 1) % 4), rel == q
-        else:
-            ahead_far, behind_far = rel == q, (rel == q) | (rel == (q + 3) % 4)
-        go_ahead = away & ahead_far if ahead_near is None else (near & ahead_near) | (away & ahead_far)
-        go_behind = away & behind_far if behind_near is None else (near & behind_near) | (away & behind_far)
-        return ((ahead, go_ahead), (behind, go_behind), (over, near & (rel == q)))
-
-    def side_each(s, q, act):
-        for way, (target, when) in enumerate(side_ways(s, q)):
-
-            @pl.when(when)
+    def side_each(s, q, u, act):
+        place = far * 4 + lax.rem(z + 4 - s, 4)
+        for way, target in enumerate((ahead, behind, over)):
+
+            @pl.when(pick(SIDE_WAYS[q][way], place) == 1)
             def _():
-                act(side_copy(s, q, way, target))
-
-    def side_relay(s, q):
-        @pl.when(c != s)
-        def _():
-            side_copy(s, q, 0, ahead).wait_recv()
-
-        side_each(s, q, lambda copy: copy.start())
-
-    def side_source(s):
-        @pl.when(c == s)
-        def _():
-            side[s] = a_ref[0]
-
-    order = (1, 3, 0, 2)
-
-    side_source(0)
-    side_source(1)
-
-    @pl.when(r < 2)
-    def _():
-        panel[core, 0] = a_ref[0]
-        panel[core, 1] = a_ref[1]
-
-    for q in order:
-        side_relay(0, q)
-
-    @pl.when(r < 2)
-    def _():
-        for half in range(4):
-            wide_start(half)
-
-    @pl.when(r >= 2)
-    def _():
-        lax.fori_loop(0, 4, lambda half, carry: (wide_relay(half), carry)[1], 0)
-
-    for q in order:
-        side_relay(1, q)
-
-    @pl.when(r == 0)
-    def _():
-        panel[0, 2] = side[1]
-
-    @pl.when(r == 1)
-    def _():
-        panel[1, 2] = side[0]
-
-    @pl.when(r < 2)
-    def _():
-        for half in (4, 5):
-            wide_start(half)
-
-    @pl.when(r >= 2)
-    def _():
-        lax.fori_loop(4, 6, lambda half, carry: (wide_relay(half), carry)[1], 0)
+                act(side_copy(s, q, u, way, target))
+
+    def side_slot(slot):
+        for s in range(2):
+            place = far * 4 + lax.rem(z + 4 - s, 4)
+            for q in (1, 3, 0, 2):
+                at = slot - 4 * s - (1 if q % 2 == 0 else 0) - SLOTS * pick(SIDE_DEPTH[q], place)
+
+                @pl.when((at == 0) | (at == 2))
+                def _():
+                    u = lax.div(at, 2)
+
+                    @pl.when(c != s)
+                    def _():
+                        side_copy(s, q, u, 0, ahead).wait_recv()
+
+                    side_each(s, q, u, start)
+
+    SIDE_END = 8 + 5 * SLOTS
 
     def put(index, value):
         high, low = split(value)
@@ -382,30 +366,7 @@
     def times(i, j):
         return product(ph[i], pl_[i], ph[j], pl_[j])
 
-    @pl.when(r == 0)
-    def _():
-        pivot[...] = side[0]
-
-    @pl.when(r >= 1)
-    def _():
-        @pl.when(core == 0)
-        def _():
-            lax.fori_loop(6, 8, lambda half, carry: (wide_relay(half), carry)[1], 0)
-
-        @pl.when(core == 1)
-        def _():
-            pair_wait(0, 8)
-
-        put(0, panel[0, 3])
-        put(1, panel[0, 2])
-        put(2, times(0, 1))
-        put(3, side[0])
-        reduced = side[1] - times(3, 2)
-        pivot[...] = reduced
-        put(4, reduced)
-
-    @pl.when(r < 2)
-    def _():
+    def invert(hook):
         here = lax.broadcasted_iota(jnp.int32, (B, B), 0) == lax.broadcasted_iota(jnp.int32, (B, B), 1)
         block = pivot[...]
         only = jnp.where(here, block, 0.0)
@@ -424,7 +385,7 @@
         sh[1, :B] = high
         sl[1, :B] = low
 
-        def step(k, carry):
+        def step(k):
             now = lax.rem(k, 2)
             later = 1 - now
             both = product(sh[now], sl[now], sh[now, B:], sl[now, B:])
@@ -436,55 +397,135 @@
             high, low = split(both[B:])
             sh[later, B:] = high
             sl[later, B:] = low
-            return carry
-
-        lax.fori_loop(1, NS_STEPS - 1, step, 0)
+            hook(k)
+
+        loop(1, NS_STEPS - 1, step)
         now = (NS_STEPS - 1) % 2
-        panel[core, 3] = xf[...] + product(sh[now, :B], sl[now, :B], sh[now, B:], sl[now, B:])
-        for half in (6, 7):
-            wide_start(half)
+        return xf[...] + product(sh[now, :B], sl[now, :B], sh[now, B:], sl[now, B:])
+
+    last_copy = pltpu.make_async_remote_copy(
+        src_ref=side.at[1],
+        dst_ref=last,
+        send_sem=last_sem.at[0],
+        recv_sem=last_sem.at[1],
+        device_id=pair,
+        device_id_type=MESH,
+    )
+
+    for s in range(2):
+
+        @pl.when(c == s)
+        def _():
+            side[s] = a_ref[0]
+
+    @pl.when(r < 2)
+    def _():
+        panel[core, 0] = a_ref[0]
+        panel[core, 1] = a_ref[1]
+        wide_source(0, 16, start)
+        pair_copy(0).start()
+        pair_copy(1).start()
 
     @pl.when(r == 0)
     def _():
-        put(0, panel[0, 3])
+        loop(0, SIDE_END - 4, side_slot)
+        pivot[...] = side[0]
+        first = invert(lambda k: side_slot(SIDE_END - 5 + k))
+        panel[0, 3] = first
+        wide_source(24, 32, start)
+        pair_copy(3).start()
+        panel[0, 2] = side[1]
+        wide_source(16, 24, start)
+        pair_copy(2).start()
+        put(0, first)
+        put(1, side[1])
+        put(2, times(0, 1))
+        pair_wait(2)
+        put(3, panel[1, 2])
+        last_copy.wait_recv()
+        pivot[...] = last[...] - times(3, 2)
+        panel[0, 4] = invert(lambda k: None)
+        wide_source(32, 40, start)
+        pair_copy(4).start()
         for j in range(2):
             put(1, a_ref[j])
             out_ref[j] = times(0, 1)
-        pair_wait(0, 8)
+        pair_wait(0)
+        pair_wait(1)
+
+    @pl.when(r == 1)
+    def _():
+        loop(0, SIDE_END, side_slot)
+        panel[1, 2] = side[0]
+        last_copy.start()
+        pair_copy(2).start()
+        wide_source(16, 24, start)
+
+    @pl.when(r >= 2)
+    def _():
+        def early(slot):
+            side_slot(slot)
+            wide_slot(0, 16, slot)
+
+        loop(0, max(SIDE_END, 6 + 4 * SLOTS), early)
+        pair_copy(0).start()
+        pair_copy(1).start()
+
+    @pl.when((r >= 2) & (core == 0))
+    def _():
+        wide_relay(24, 32)
+        pair_copy(3).start()
+        wide_relay(16, 24)
+        pair_copy(2).start()
+        pair_wait(0)
+        pair_wait(1)
+        pair_wait(2)
+
+    @pl.when((r >= 2) & (core == 1))
+    def _():
+        wide_relay(16, 24)
+        pair_copy(2).start()
+
+    @pl.when(core == 1)
+    def _():
+        for b in range(4):
+            pair_wait(b)
 
     @pl.when(r >= 1)
     def _():
+        put(0, panel[0, 3])
+        put(3, side[0])
         for j in range(2):
             put(1, panel[0, j])
-            put(5 + j, times(0, 1))
-            kept = a_ref[j] - times(3, 5 + j)
+            put(4 + j, times(0, 1))
+            kept = a_ref[j] - times(3, 4 + j)
             out_ref[j] = kept
 
             @pl.when(r == 1)
             def _():
-                put(7 + j, kept)
+                put(6 + j, kept)
 
         @pl.when(r >= 2)
         def _():
-            @pl.when(core == 0)
-            def _():
-                pair_wait(0, 6)
-
             put(1, panel[1, 2])
             for j in range(2):
-                put(7 + j, panel[1, j] - times(1, 5 + j))
-
-            @pl.when(core == 1)
-            def _():
-                lax.fori_loop(6, 8, lambda half, carry: (wide_relay(half), carry)[1], 0)
-
-            @pl.when(core == 0)
-            def _():
-                pair_wait(6, 8)
-
-        put(0, panel[1, 3])
+                put(6 + j, panel[1, j] - times(1, 4 + j))
+            put(1, panel[0, 2])
+            put(2, times(0, 1))
+            put(4, side[1] - times(3, 2))
+
+        @pl.when((r >= 2) & (core == 0))
+        def _():
+            wide_relay(32, 40)
+            pair_copy(4).start()
+
+        @pl.when(core == 1)
+        def _():
+            pair_wait(4)
+
+        put(0, panel[0, 4])
         for j in range(2):
-            scaled = times(0, 7 + j)
+            scaled = times(0, 6 + j)
             live = c >= 2 if j == 0 else c >= 0
 
             @pl.when((r == 1) & live)
@@ -500,15 +541,26 @@
     def _():
         out_ref[0] = a_ref[0]
 
-    def sent(half, carry):
-        for tree in range(3):
-            each_way(half, tree, lambda copy: copy.wait_send())
-        return carry
-
-    lax.fori_loop(0, 8, sent, 0)
     for s in range(2):
         for q in range(4):
-            side_each(s, q, lambda copy: copy.wait_send())
+            for u in range(2):
+                side_each(s, q, u, sent)
+
+    @pl.when(core == 0)
+    def _():
+        wide_source(0, 40, sent)
+        for b in range(5):
+            pair_copy(b).wait_send()
+
+    @pl.when(core == 1)
+    def _():
+        wide_source(0, 24, sent)
+        for b in range(3):
+            pair_copy(b).wait_send()
+
+    @pl.when(r == 1)
+    def _():
+        last_copy.wait_send()
 
 
 def eliminate(blocks):
@@ -521,18 +573,21 @@
         out_specs=vmem,
         scratch_shapes=[
             pltpu.VMEM((2, B, B), F32),
-            pltpu.VMEM((2, 4, B, B), F32),
+            pltpu.VMEM((2, 5, B, B), F32),
             pltpu.VMEM((B, B), F32),
-            pltpu.VMEM((9, B, B), BF16),
-            pltpu.VMEM((9, B, B), BF16),
+            pltpu.VMEM((B, B), F32),
+            pltpu.VMEM((8, B, B), BF16),
+            pltpu.VMEM((8, B, B), BF16),
             pltpu.VMEM((2, 2 * B, B), BF16),
             pltpu.VMEM((2, 2 * B, B), BF16),
             pltpu.VMEM((B, B), F32),
-            dma((24, 4)),
-            dma((24,)),
-            dma((24,)),
-            dma((2, 4, 3)),
-            dma((2, 4)),
+            dma((40, 3)),
+            dma((40,)),
+            dma((5,)),
+            dma((5,)),
+            dma((2, 4, 2, 3)),
+            dma((2, 4, 2)),
+            dma((2,)),
         ],
         compiler_params=pltpu.CompilerParams(
             collective_id=1, has_side_effects=True, vmem_limit_bytes=VMEM_LIMIT

time: 433 us -> 144 us (0.33); the launches traced: 428 us -> 143 us
  Pallas kernels: 422 us -> 137 us
    pallas_call x1, Pallas kernels: 405 us -> 121 us  [eliminate(): pl.pallas_call(eliminate_kernel, out_shape=jax.ShapeDtypeStruct((2, B, B)...]
where the time goes in v3:
time: 144 us; the launch traced here: 143 us
  Pallas kernels  137 us (95%)
  local copies, waits for them, and re-layouts  5.89 us (4%)
    pallas_call x1, Pallas kernels, eliminate(): pl.pallas_call(eliminate_kernel, out_shape=jax.ShapeDtypeStruct((2, B, B)...  121 us
    pallas_call x1, Pallas kernels, gather_heads(): pl.pallas_call(gather_heads_kernel, out_shape=jax.ShapeDtypeStruct((64, L...  9.79 us
    pallas_call x1, Pallas kernels, add_weirs(): pl.pallas_call(weirs_kernel, out_shape=jax.ShapeDtypeStruct((2, B, B), F3...  6.64 us
    unnamed x1, local copies, waits for them, and re-layouts  3.08 us

profile of v3, /device:TPU:21, one launch (start us, length us, event | category | flops | bytes accessed | tf_op | source)
XLA Modules:
  0.0 143.2 jit_solution(2685513225779727687)
XLA Ops:
  0.0 9.8 %gather_heads.1.heads_ref = f32[64,128]{1,0:T(8,128)} custom-call(f32[8,128]{1,0:T(8,128)} %bitcast.13), custom_call_target="tpu_custom_call" | custom-call | tf_op jit(solution)/shard_map/gather_heads/pallas_call | solution.py:78
  9.8 1.4 pad_bitcast_fusion.2.coef_ref
  11.2 1.4 pad_bitcast_fusion
  12.6 6.6 %add_weirs.1.a_ref = f32[2,512,512]{2,1,0:T(8,128)} custom-call(s32[16,16]{1,0:T(8,128)} %mask_ref.1, f32[2,512,512]{2,1,0:T(8,128)} %bitcast.12, f32[64,128]{1,0:T(8,128)} %gather_heads.1.heads_ref, f32[72,128]{1,0:T(8,128)} %pad_bitcast_fusion.2.coef_ref, s32[72,128]{1,0:T(8,128)} %get-tuple-element.6.node_ref, s32[72,128]{1,0:T(8,128)} %get-tuple-element.5.cell_ref), custom_call_target="tpu_custom_call" | custom-call | tf_op jit(solution)/shard_map/add_weirs/pallas_call | solution.py:197
  19.2 120.8 %eliminate.1 = f32[2,512,512]{2,1,0:T(8,128)} custom-call(f32[2,512,512]{2,1,0:T(8,128)} %add_weirs.1.a_ref), custom_call_target="tpu_custom_call" | custom-call | tf_op jit(solution)/shard_map/eliminate/pallas_call | solution.py:569
  140.1 3.1 %copy.9 = f32[1,1,2,1,512,512]{5,4,3,2,1,0:T(8,128)} copy(f32[1,1,2,1,512,512]{5,4,3,2,1,0:T(8,128)} %bitcast.11) | data formatting | bytes 4194304

commit v4 on v3

--- a/solution.py
+++ b/solution.py
@@ -16,18 +16,13 @@
 BF16 = jnp.bfloat16
 VMEM_LIMIT = 56 * 2**20
 SLOTS = 2
-WIDE_DEPTH = ((0, 1, 2, 3, 3, 2, 3, 4), (0, 3, 2, 1, 3, 4, 3, 2), (0, 3, 4, 3, 1, 2, 3, 2))
-WIDE_WAYS = (
+CHUNK = 32
+PARTS = B // CHUNK
+TREE_DEPTH = ((0, 1, 2, 3, 3, 2, 3, 4), (0, 3, 2, 1, 3, 4, 3, 2), (0, 3, 4, 3, 1, 2, 3, 2))
+TREE_WAYS = (
     ((1, 1, 1, 0, 0, 0, 1, 0), (0, 0, 0, 0, 0, 1, 0, 0), (0, 1, 1, 0, 0, 0, 0, 0)),
     ((0, 0, 0, 0, 0, 0, 0, 1), (1, 0, 1, 1, 0, 0, 1, 1), (0, 0, 0, 1, 0, 0, 0, 0)),
     ((0, 0, 0, 0, 1, 1, 0, 0), (0, 0, 0, 0, 1, 0, 0, 0), (1, 0, 0, 0, 0, 1, 1, 1)),
-)
-SIDE_DEPTH = ((0, 1, 2, 3, 1, 2, 3, 2), (0, 1, 2, 3, 3, 2, 3, 4), (0, 3, 2, 1, 5, 4, 3, 4), (0, 3, 2, 1, 3, 4, 3, 2))
-SIDE_WAYS = (
-    ((1, 1, 1, 0, 1, 1, 0, 0), (0, 0, 0, 0, 1, 0, 0, 0), (1, 0, 0, 0, 0, 0, 0, 0)),
-    ((1, 1, 1, 0, 0, 1, 0, 0), (0, 0, 0, 0, 1, 1, 0, 0), (0, 1, 0, 0, 0, 0, 0, 0)),
-    ((0, 0, 0, 0, 0, 0, 1, 1), (1, 0, 1, 1, 0, 0, 1, 0), (0, 0, 1, 0, 0, 0, 0, 0)),
-    ((0, 0, 0, 0, 0, 0, 0, 1), (1, 0, 1, 1, 0, 0, 1, 1), (0, 0, 0, 1, 0, 0, 0, 0)),
 )
 
 
@@ -210,7 +205,7 @@
     out_ref,
     side,
     panel,
-    last,
+    corner,
     pivot,
     ph,
     pl_,
@@ -223,7 +218,9 @@
     pair_recv,
     side_send,
     side_recv,
-    last_sem,
+    corner_sem,
+    last_send,
+    last_recv,
 ):
     r = lax.axis_index("wide")
     c = lax.axis_index("narrow")
@@ -255,12 +252,12 @@
     start = lambda copy: copy.start()
     sent = lambda copy: copy.wait_send()
 
-    depth = tuple(pick(values, chip) for values in WIDE_DEPTH)
-    ways = tuple(tuple(pick(values, chip) == 1 for values in tree) for tree in WIDE_WAYS)
+    depth = tuple(pick(values, chip) for values in TREE_DEPTH)
+    ways = tuple(tuple(pick(values, chip) == 1 for values in tree) for tree in TREE_WAYS)
 
     def wide_copy(j, way, target):
-        rows = pl.ds(pl.multiple_of(lax.rem(j, 8) * 64, 64), 64)
-        chunk = panel.at[core, lax.div(j, 8), rows]
+        rows = pl.ds(pl.multiple_of(lax.rem(j, PARTS) * CHUNK, CHUNK), CHUNK)
+        chunk = panel.at[core, lax.div(j, PARTS), rows]
         return pltpu.make_async_remote_copy(
             src_ref=chunk,
             dst_ref=chunk,
@@ -277,7 +274,7 @@
             def _():
                 act(wide_copy(j, way, target))
 
-    def wide_slot(first, end, slot):
+    def wide_slot(first, end, slot, forward=False):
         for tree in range(3):
             j = 3 * (slot - SLOTS * depth[tree]) + tree
 
@@ -285,11 +282,14 @@
             def _():
                 wide_copy(j, 0, up).wait_recv()
                 wide_each(tree, j, start)
-
-    def wide_relay(first, end):
-        loop(first // 3 - 1, (end + 2) // 3 + 4 * SLOTS, lambda slot: wide_slot(first, end, slot))
-
-    def wide_source(first, end, act):
+                if forward:
+                    last_copy(j).start()
+
+    def wide_relay(block, forward=False):
+        first, end = block * PARTS, (block + 1) * PARTS
+        loop(first // 3 - 1, (end + 2) // 3 + 4 * SLOTS, lambda slot: wide_slot(first, end, slot, forward))
+
+    def wide_source(block, act):
         def one(j):
             for tree in range(3):
 
@@ -297,7 +297,7 @@
                 def _():
                     wide_each(tree, j, act)
 
-        loop(first, end, one)
+        loop(block * PARTS, (block + 1) * PARTS, one)
 
     def pair_copy(b):
         block = panel.at[core, b]
@@ -321,42 +321,57 @@
             device_id_type=MESH,
         ).wait_recv()
 
-    def side_copy(s, q, u, way, target):
-        chunk = side.at[s, pl.ds(pl.multiple_of(q * 128 + u * 64, 64), 64)]
+    def last_copy(j):
+        rows = pl.ds(pl.multiple_of(lax.rem(j, PARTS) * CHUNK, CHUNK), CHUNK)
+        chunk = panel.at[0, 4, rows]
         return pltpu.make_async_remote_copy(
             src_ref=chunk,
             dst_ref=chunk,
-            send_sem=side_send.at[s, q, u, way],
-            recv_sem=side_recv.at[s, q, u],
+            send_sem=last_send.at[lax.rem(j, PARTS)],
+            recv_sem=last_recv.at[lax.rem(j, PARTS)],
+            device_id=pair,
+            device_id_type=MESH,
+        )
+
+    def side_copy(s, j, way, target):
+        chunk = side.at[s, pl.ds(pl.multiple_of(j * CHUNK, CHUNK), CHUNK)]
+        return pltpu.make_async_remote_copy(
+            src_ref=chunk,
+            dst_ref=chunk,
+            send_sem=side_send.at[s, j, way],
+            recv_sem=side_recv.at[s, j],
             device_id=target,
             device_id_type=MESH,
         )
 
-    def side_each(s, q, u, act):
-        place = far * 4 + lax.rem(z + 4 - s, 4)
+    places = tuple(far * 4 + lax.rem(z + 4 - s, 4) for s in range(2))
+    side_depth = tuple(tuple(pick(values, place) for values in TREE_DEPTH) for place in places)
+    side_ways = tuple(
+        tuple(tuple(pick(values, place) == 1 for values in tree) for tree in TREE_WAYS) for place in places
+    )
+
+    def side_each(s, tree, j, act):
         for way, target in enumerate((ahead, behind, over)):
 
-            @pl.when(pick(SIDE_WAYS[q][way], place) == 1)
+            @pl.when(side_ways[s][tree][way])
             def _():
-                act(side_copy(s, q, u, way, target))
+                act(side_copy(s, j, way, target))
 
     def side_slot(slot):
         for s in range(2):
-            place = far * 4 + lax.rem(z + 4 - s, 4)
-            for q in (1, 3, 0, 2):
-                at = slot - 4 * s - (1 if q % 2 == 0 else 0) - SLOTS * pick(SIDE_DEPTH[q], place)
-
-                @pl.when((at == 0) | (at == 2))
+            for tree in range(3):
+                j = 3 * (slot - 6 * s - SLOTS * side_depth[s][tree]) + tree
+
+                @pl.when((j >= 0) & (j < PARTS))
                 def _():
-                    u = lax.div(at, 2)
-
                     @pl.when(c != s)
                     def _():
-                        side_copy(s, q, u, 0, ahead).wait_recv()
-
-                    side_each(s, q, u, start)
-
-    SIDE_END = 8 + 5 * SLOTS
+                        side_copy(s, j, 0, ahead).wait_recv()
+
+                    side_each(s, tree, j, start)
+
+    SIDE_FIRST = 6 + 4 * SLOTS
+    SIDE_END = 12 + 4 * SLOTS
 
     def put(index, value):
         high, low = split(value)
@@ -403,11 +418,11 @@
         now = (NS_STEPS - 1) % 2
         return xf[...] + product(sh[now, :B], sl[now, :B], sh[now, B:], sl[now, B:])
 
-    last_copy = pltpu.make_async_remote_copy(
+    corner_copy = pltpu.make_async_remote_copy(
         src_ref=side.at[1],
-        dst_ref=last,
-        send_sem=last_sem.at[0],
-        recv_sem=last_sem.at[1],
+        dst_ref=corner,
+        send_sem=corner_sem.at[0],
+        recv_sem=corner_sem.at[1],
         device_id=pair,
         device_id_type=MESH,
     )
@@ -422,31 +437,40 @@
     def _():
         panel[core, 0] = a_ref[0]
         panel[core, 1] = a_ref[1]
-        wide_source(0, 16, start)
+        wide_source(0, start)
+        wide_source(1, start)
         pair_copy(0).start()
         pair_copy(1).start()
 
     @pl.when(r == 0)
     def _():
-        loop(0, SIDE_END - 4, side_slot)
+        loop(0, SIDE_FIRST, side_slot)
         pivot[...] = side[0]
-        first = invert(lambda k: side_slot(SIDE_END - 5 + k))
+
+        def between(k):
+            side_slot(SIDE_FIRST + 2 * k - 2)
+            side_slot(SIDE_FIRST + 2 * k - 1)
+
+            @pl.when(k == 4)
+            def _():
+                panel[0, 2] = side[1]
+                wide_source(2, start)
+                pair_copy(2).start()
+
+        first = invert(between)
         panel[0, 3] = first
-        wide_source(24, 32, start)
+        wide_source(3, start)
         pair_copy(3).start()
-        panel[0, 2] = side[1]
-        wide_source(16, 24, start)
-        pair_copy(2).start()
         put(0, first)
         put(1, side[1])
         put(2, times(0, 1))
         pair_wait(2)
         put(3, panel[1, 2])
-        last_copy.wait_recv()
-        pivot[...] = last[...] - times(3, 2)
+        corner_copy.wait_recv()
+        pivot[...] = corner[...] - times(3, 2)
         panel[0, 4] = invert(lambda k: None)
-        wide_source(32, 40, start)
-        pair_copy(4).start()
+        wide_source(4, start)
+        loop(0, PARTS, lambda j: last_copy(j).start())
         for j in range(2):
             put(1, a_ref[j])
             out_ref[j] = times(0, 1)
@@ -457,33 +481,33 @@
     def _():
         loop(0, SIDE_END, side_slot)
         panel[1, 2] = side[0]
-        last_copy.start()
+        corner_copy.start()
         pair_copy(2).start()
-        wide_source(16, 24, start)
+        wide_source(2, start)
 
     @pl.when(r >= 2)
     def _():
         def early(slot):
             side_slot(slot)
-            wide_slot(0, 16, slot)
-
-        loop(0, max(SIDE_END, 6 + 4 * SLOTS), early)
+            wide_slot(0, 2 * PARTS, slot)
+
+        loop(0, max(SIDE_END, 11 + 4 * SLOTS), early)
         pair_copy(0).start()
         pair_copy(1).start()
 
     @pl.when((r >= 2) & (core == 0))
     def _():
-        wide_relay(24, 32)
+        wide_relay(2)
+        pair_copy(2).start()
+        wide_relay(3)
         pair_copy(3).start()
-        wide_relay(16, 24)
-        pair_copy(2).start()
         pair_wait(0)
         pair_wait(1)
         pair_wait(2)
 
     @pl.when((r >= 2) & (core == 1))
     def _():
-        wide_relay(16, 24)
+        wide_relay(2)
         pair_copy(2).start()
 
     @pl.when(core == 1)
@@ -516,12 +540,11 @@
 
         @pl.when((r >= 2) & (core == 0))
         def _():
-            wide_relay(32, 40)
-            pair_copy(4).start()
+            wide_relay(4, forward=True)
 
         @pl.when(core == 1)
         def _():
-            pair_wait(4)
+            loop(0, PARTS, lambda j: last_copy(j).wait_recv())
 
         put(0, panel[0, 4])
         for j in range(2):
@@ -542,25 +565,33 @@
         out_ref[0] = a_ref[0]
 
     for s in range(2):
-        for q in range(4):
-            for u in range(2):
-                side_each(s, q, u, sent)
+
+        def one(j):
+            for tree in range(3):
+
+                @pl.when(lax.rem(j, 3) == tree)
+                def _():
+                    side_each(s, tree, j, sent)
+
+        loop(0, PARTS, one)
 
     @pl.when(core == 0)
     def _():
-        wide_source(0, 40, sent)
         for b in range(5):
+            wide_source(b, sent)
+        for b in range(4):
             pair_copy(b).wait_send()
+        loop(0, PARTS, lambda j: last_copy(j).wait_send())
 
     @pl.when(core == 1)
     def _():
-        wide_source(0, 24, sent)
         for b in range(3):
+            wide_source(b, sent)
             pair_copy(b).wait_send()
 
     @pl.when(r == 1)
     def _():
-        last_copy.wait_send()
+        corner_copy.wait_send()
 
 
 def eliminate(blocks):
@@ -581,13 +612,15 @@
             pltpu.VMEM((2, 2 * B, B), BF16),
             pltpu.VMEM((2, 2 * B, B), BF16),
             pltpu.VMEM((B, B), F32),
-            dma((40, 3)),
-            dma((40,)),
-            dma((5,)),
-            dma((5,)),
-            dma((2, 4, 2, 3)),
-            dma((2, 4, 2)),
+            dma((5 * PARTS, 3)),
+            dma((5 * PARTS,)),
+            dma((4,)),
+            dma((4,)),
+            dma((2, PARTS, 3)),
+            dma((2, PARTS)),
             dma((2,)),
+            dma((PARTS,)),
+            dma((PARTS,)),
         ],
         compiler_params=pltpu.CompilerParams(
             collective_id=1, has_side_effects=True, vmem_limit_bytes=VMEM_LIMIT

time: 144 us -> 153 us (1.062)
  Pallas kernels: 137 us -> 146 us
    pallas_call x1, Pallas kernels: 121 us -> 130 us  [eliminate(): pl.pallas_call(eliminate_kernel, out_shape=jax.ShapeDtypeStruct((2, B, B)...]
where the time goes in v4:
time: 153 us; the launch traced here: 152 us
  Pallas kernels  146 us (95%)
  local copies, waits for them, and re-layouts  5.89 us (4%)
    pallas_call x1, Pallas kernels, eliminate(): pl.pallas_call(eliminate_kernel, out_shape=jax.ShapeDtypeStruct((2, B, B)...  130 us
    pallas_call x1, Pallas kernels, gather_heads(): pl.pallas_call(gather_heads_kernel, out_shape=jax.ShapeDtypeStruct((64, L...  9.79 us
    pallas_call x1, Pallas kernels, add_weirs(): pl.pallas_call(weirs_kernel, out_shape=jax.ShapeDtypeStruct((2, B, B), F3...  6.64 us
    unnamed x1, local copies, waits for them, and re-layouts  3.08 us

profile of v4, /device:TPU:21, one launch (start us, length us, event | category | flops | bytes accessed | tf_op | source)
XLA Modules:
  0.0 151.9 jit_solution(3540221404355390455)
XLA Ops:
  0.0 9.8 %gather_heads.1.heads_ref = f32[64,128]{1,0:T(8,128)} custom-call(f32[8,128]{1,0:T(8,128)} %bitcast.13), custom_call_target="tpu_custom_call" | custom-call | tf_op jit(solution)/shard_map/gather_heads/pallas_call | solution.py:73
  9.8 1.4 pad_bitcast_fusion.2.coef_ref
  11.2 1.4 pad_bitcast_fusion
  12.6 6.6 %add_weirs.1.a_ref = f32[2,512,512]{2,1,0:T(8,128)} custom-call(s32[16,16]{1,0:T(8,128)} %mask_ref.1, f32[2,512,512]{2,1,0:T(8,128)} %bitcast.12, f32[64,128]{1,0:T(8,128)} %gather_heads.1.heads_ref, f32[72,128]{1,0:T(8,128)} %pad_bitcast_fusion.2.coef_ref, s32[72,128]{1,0:T(8,128)} %get-tuple-element.6.node_ref, s32[72,128]{1,0:T(8,128)} %get-tuple-element.5.cell_ref), custom_call_target="tpu_custom_call" | custom-call | tf_op jit(solution)/shard_map/add_weirs/pallas_call | solution.py:192
  19.2 129.6 %eliminate.1 = f32[2,512,512]{2,1,0:T(8,128)} custom-call(f32[2,512,512]{2,1,0:T(8,128)} %add_weirs.1.a_ref), custom_call_target="tpu_custom_call" | custom-call | tf_op jit(solution)/shard_map/eliminate/pallas_call | solution.py:600
  148.8 3.1 %copy.9 = f32[1,1,2,1,512,512]{5,4,3,2,1,0:T(8,128)} copy(f32[1,1,2,1,512,512]{5,4,3,2,1,0:T(8,128)} %bitcast.11) | data formatting | bytes 4194304

commit v5 on v4

--- a/solution.py
+++ b/solution.py
@@ -16,7 +16,7 @@
 BF16 = jnp.bfloat16
 VMEM_LIMIT = 56 * 2**20
 SLOTS = 2
-CHUNK = 32
+CHUNK = 64
 PARTS = B // CHUNK
 TREE_DEPTH = ((0, 1, 2, 3, 3, 2, 3, 4), (0, 3, 2, 1, 3, 4, 3, 2), (0, 3, 4, 3, 1, 2, 3, 2))
 TREE_WAYS = (
@@ -205,7 +205,7 @@
     out_ref,
     side,
     panel,
-    corner,
+    direct,
     pivot,
     ph,
     pl_,
@@ -218,7 +218,10 @@
     pair_recv,
     side_send,
     side_recv,
-    corner_sem,
+    direct_send,
+    direct_recv,
+    inverse_send,
+    inverse_recv,
     last_send,
     last_recv,
 ):
@@ -285,8 +288,8 @@
                 if forward:
                     last_copy(j).start()
 
-    def wide_relay(block, forward=False):
-        first, end = block * PARTS, (block + 1) * PARTS
+    def wide_relay(first_block, end_block, forward=False):
+        first, end = first_block * PARTS, end_block * PARTS
         loop(first // 3 - 1, (end + 2) // 3 + 4 * SLOTS, lambda slot: wide_slot(first, end, slot, forward))
 
     def wide_source(block, act):
@@ -323,7 +326,7 @@
 
     def last_copy(j):
         rows = pl.ds(pl.multiple_of(lax.rem(j, PARTS) * CHUNK, CHUNK), CHUNK)
-        chunk = panel.at[0, 4, rows]
+        chunk = panel.at[0, 3, rows]
         return pltpu.make_async_remote_copy(
             src_ref=chunk,
             dst_ref=chunk,
@@ -345,22 +348,24 @@
         )
 
     places = tuple(far * 4 + lax.rem(z + 4 - s, 4) for s in range(2))
-    side_depth = tuple(tuple(pick(values, place) for values in TREE_DEPTH) for place in places)
-    side_ways = tuple(
-        tuple(tuple(pick(values, place) == 1 for values in tree) for tree in TREE_WAYS) for place in places
-    )
+    side_depth = [[pick(values, place) for values in TREE_DEPTH] for place in places]
+    side_ways = [
+        [[pick(values, place) for values in tree] for tree in TREE_WAYS] for place in places
+    ]
+    side_depth[1][1] = jnp.where(r == 0, side_depth[1][2], side_depth[1][1])
+    side_ways[1][1] = [jnp.where(r == 0, v2, v1) for v1, v2 in zip(side_ways[1][1], side_ways[1][2])]
 
     def side_each(s, tree, j, act):
         for way, target in enumerate((ahead, behind, over)):
 
-            @pl.when(side_ways[s][tree][way])
+            @pl.when(side_ways[s][tree][way] == 1)
             def _():
                 act(side_copy(s, j, way, target))
 
-    def side_slot(slot):
-        for s in range(2):
+    def side_slot(slot, panels):
+        for s in panels:
             for tree in range(3):
-                j = 3 * (slot - 6 * s - SLOTS * side_depth[s][tree]) + tree
+                j = 3 * (slot - 3 * s - SLOTS * side_depth[s][tree]) + tree
 
                 @pl.when((j >= 0) & (j < PARTS))
                 def _():
@@ -370,8 +375,48 @@
 
                     side_each(s, tree, j, start)
 
-    SIDE_FIRST = 6 + 4 * SLOTS
-    SIDE_END = 12 + 4 * SLOTS
+    SIDE_END = 6 + 4 * SLOTS
+
+    def inverse_copy(b, j, way, target):
+        chunk = panel.at[0, b, pl.ds(pl.multiple_of(j * CHUNK, CHUNK), CHUNK)]
+        return pltpu.make_async_remote_copy(
+            src_ref=chunk,
+            dst_ref=chunk,
+            send_sem=inverse_send.at[b - 2, j, way],
+            recv_sem=inverse_recv.at[b - 2, j],
+            device_id=target,
+            device_id_type=MESH,
+        )
+
+    def inverse_each(b, tree, j, act):
+        for way, target in enumerate((ahead, behind, over)):
+
+            @pl.when(side_ways[0][tree][way] == 1)
+            def _():
+                act(inverse_copy(b, j, way, target))
+
+    def inverse_slot(b, slot):
+        for tree in range(3):
+            j = 3 * (slot - SLOTS * side_depth[0][tree]) + tree
+
+            @pl.when((j >= 0) & (j < PARTS))
+            def _():
+                @pl.when(c != 0)
+                def _():
+                    inverse_copy(b, j, 0, ahead).wait_recv()
+
+                inverse_each(b, tree, j, start)
+                for kind in range(3):
+
+                    @pl.when(lax.rem(b * PARTS + j, 3) == kind)
+                    def _():
+                        wide_each(kind, b * PARTS + j, start)
+
+    INVERSE_LATER = 4
+    INVERSE_END = (PARTS + 2) // 3 + 4 * SLOTS
+
+    def inverse_pass(b):
+        loop(0, INVERSE_END, lambda slot: inverse_slot(b, slot))
 
     def put(index, value):
         high, low = split(value)
@@ -381,7 +426,7 @@
     def times(i, j):
         return product(ph[i], pl_[i], ph[j], pl_[j])
 
-    def invert(hook):
+    def invert():
         here = lax.broadcasted_iota(jnp.int32, (B, B), 0) == lax.broadcasted_iota(jnp.int32, (B, B), 1)
         block = pivot[...]
         only = jnp.where(here, block, 0.0)
@@ -412,20 +457,26 @@
             high, low = split(both[B:])
             sh[later, B:] = high
             sl[later, B:] = low
-            hook(k)
 
         loop(1, NS_STEPS - 1, step)
         now = (NS_STEPS - 1) % 2
         return xf[...] + product(sh[now, :B], sl[now, :B], sh[now, B:], sl[now, B:])
 
-    corner_copy = pltpu.make_async_remote_copy(
-        src_ref=side.at[1],
-        dst_ref=corner,
-        send_sem=corner_sem.at[0],
-        recv_sem=corner_sem.at[1],
-        device_id=pair,
-        device_id_type=MESH,
-    )
+    def direct_copy(src, dst, at, target):
+        return pltpu.make_async_remote_copy(
+            src_ref=src,
+            dst_ref=dst,
+            send_sem=direct_send.at[at],
+            recv_sem=direct_recv.at[at],
+            device_id=target,
+            device_id_type=MESH,
+        )
+
+    first_copy = direct_copy(side.at[1], direct.at[0], 0, behind)
+    second_copy = direct_copy(direct.at[1], direct.at[1], 1, behind)
+    corner_copy = direct_copy(side.at[1], direct.at[1], 2, pair)
+    cross_copy = direct_copy(side.at[1], panel.at[1, 3], 3, pair)
+    cross_first = direct_copy(direct.at[0], panel.at[1, 3], 3, pair)
 
     for s in range(2):
 
@@ -442,82 +493,114 @@
         pair_copy(0).start()
         pair_copy(1).start()
 
-    @pl.when(r == 0)
-    def _():
-        loop(0, SIDE_FIRST, side_slot)
+    @pl.when((r == 1) & (c == 1))
+    def _():
+        corner_copy.start()
+
+    @pl.when((r == 0) & (c == 1))
+    def _():
+        first_copy.start()
+        corner_copy.wait_recv()
+        second_copy.start()
+
+    @pl.when((r == 0) & (c == 0))
+    def _():
         pivot[...] = side[0]
-
-        def between(k):
-            side_slot(SIDE_FIRST + 2 * k - 2)
-            side_slot(SIDE_FIRST + 2 * k - 1)
-
-            @pl.when(k == 4)
-            def _():
-                panel[0, 2] = side[1]
-                wide_source(2, start)
-                pair_copy(2).start()
-
-        first = invert(between)
-        panel[0, 3] = first
-        wide_source(3, start)
-        pair_copy(3).start()
+        first = invert()
+        panel[0, 2] = first
+        inverse_pass(2)
+        pair_copy(2).start()
         put(0, first)
-        put(1, side[1])
+        first_copy.wait_recv()
+        cross_first.start()
+        put(1, direct[0])
         put(2, times(0, 1))
         pair_wait(2)
         put(3, panel[1, 2])
-        corner_copy.wait_recv()
-        pivot[...] = corner[...] - times(3, 2)
-        panel[0, 4] = invert(lambda k: None)
-        wide_source(4, start)
+        second_copy.wait_recv()
+        pivot[...] = direct[1] - times(3, 2)
+        panel[0, 3] = invert()
+        inverse_pass(3)
         loop(0, PARTS, lambda j: last_copy(j).start())
+        loop(0, SIDE_END, lambda slot: side_slot(slot, (1,)))
+
+    @pl.when((r == 0) & (c != 0))
+    def _():
+        def both(slot):
+            side_slot(slot, (1,))
+
+            @pl.when(slot == SIDE_END - 1)
+            def _():
+                cross_copy.start()
+
+            inverse_slot(2, slot - INVERSE_LATER)
+
+        loop(0, INVERSE_END + INVERSE_LATER, both)
+        pair_copy(2).start()
+        inverse_pass(3)
+        loop(0, PARTS, lambda j: last_copy(j).start())
+        pair_wait(2)
+
+    @pl.when(r == 0)
+    def _():
+        put(0, panel[0, 2])
         for j in range(2):
             put(1, a_ref[j])
             out_ref[j] = times(0, 1)
         pair_wait(0)
         pair_wait(1)
+        pair_wait(3)
 
     @pl.when(r == 1)
     def _():
-        loop(0, SIDE_END, side_slot)
-        panel[1, 2] = side[0]
-        corner_copy.start()
-        pair_copy(2).start()
+        @pl.when(c == 0)
+        def _():
+            panel[1, 2] = side[0]
+            pair_copy(2).start()
+
+        loop(0, SIDE_END, lambda slot: side_slot(slot, (0,)))
+
+        @pl.when(c != 0)
+        def _():
+            panel[1, 2] = side[0]
+            pair_copy(2).start()
+
         wide_source(2, start)
+        cross_copy.wait_recv()
+        wide_source(3, start)
+        pair_copy(3).start()
 
     @pl.when(r >= 2)
     def _():
         def early(slot):
-            side_slot(slot)
+            side_slot(slot, (0, 1))
             wide_slot(0, 2 * PARTS, slot)
 
-        loop(0, max(SIDE_END, 11 + 4 * SLOTS), early)
+        loop(0, SIDE_END, early)
         pair_copy(0).start()
         pair_copy(1).start()
 
     @pl.when((r >= 2) & (core == 0))
     def _():
-        wide_relay(2)
+        wide_relay(2, 3)
         pair_copy(2).start()
-        wide_relay(3)
+        for b in range(3):
+            pair_wait(b)
+
+    @pl.when((r >= 2) & (core == 1))
+    def _():
+        wide_relay(2, 4)
+        pair_copy(2).start()
         pair_copy(3).start()
-        pair_wait(0)
-        pair_wait(1)
-        pair_wait(2)
-
-    @pl.when((r >= 2) & (core == 1))
-    def _():
-        wide_relay(2)
-        pair_copy(2).start()
 
     @pl.when(core == 1)
     def _():
-        for b in range(4):
+        for b in range(3):
             pair_wait(b)
 
     @pl.when(r >= 1)
     def _():
-        put(0, panel[0, 3])
+        put(0, panel[0, 2])
         put(3, side[0])
         for j in range(2):
             put(1, panel[0, j])
@@ -534,19 +617,24 @@
             put(1, panel[1, 2])
             for j in range(2):
                 put(6 + j, panel[1, j] - times(1, 4 + j))
-            put(1, panel[0, 2])
+
+            @pl.when(core == 0)
+            def _():
+                pair_wait(3)
+
+            put(1, panel[1, 3])
             put(2, times(0, 1))
             put(4, side[1] - times(3, 2))
 
         @pl.when((r >= 2) & (core == 0))
         def _():
-            wide_relay(4, forward=True)
+            wide_relay(3, 4, forward=True)
 
         @pl.when(core == 1)
         def _():
             loop(0, PARTS, lambda j: last_copy(j).wait_recv())
 
-        put(0, panel[0, 4])
+        put(0, panel[0, 3])
         for j in range(2):
             scaled = times(0, 6 + j)
             live = c >= 2 if j == 0 else c >= 0
@@ -564,8 +652,7 @@
     def _():
         out_ref[0] = a_ref[0]
 
-    for s in range(2):
-
+    def side_sent(s):
         def one(j):
             for tree in range(3):
 
@@ -575,21 +662,46 @@
 
         loop(0, PARTS, one)
 
+    @pl.when(r >= 1)
+    def _():
+        side_sent(0)
+
+    @pl.when(r != 1)
+    def _():
+        side_sent(1)
+
+    @pl.when(r == 0)
+    def _():
+        def one(j):
+            for tree in range(3):
+
+                @pl.when(lax.rem(j, 3) == tree)
+                def _():
+                    inverse_each(2, tree, j, sent)
+                    inverse_each(3, tree, j, sent)
+
+        loop(0, PARTS, one)
+        cross_copy.wait_send()
+
+        @pl.when(c == 1)
+        def _():
+            first_copy.wait_send()
+            second_copy.wait_send()
+
+    for b in range(4):
+        wide_source(b, sent)
+    for b in range(3):
+        pair_copy(b).wait_send()
+
     @pl.when(core == 0)
     def _():
-        for b in range(5):
-            wide_source(b, sent)
-        for b in range(4):
-            pair_copy(b).wait_send()
         loop(0, PARTS, lambda j: last_copy(j).wait_send())
 
     @pl.when(core == 1)
     def _():
-        for b in range(3):
-            wide_source(b, sent)
-            pair_copy(b).wait_send()
-
-    @pl.when(r == 1)
+        pair_copy(3).wait_send()
+
+    @pl.when((r == 1) & (c == 1))
     def _():
         corner_copy.wait_send()
 
@@ -604,21 +716,24 @@
         out_specs=vmem,
         scratch_shapes=[
             pltpu.VMEM((2, B, B), F32),
-            pltpu.VMEM((2, 5, B, B), F32),
-            pltpu.VMEM((B, B), F32),
+            pltpu.VMEM((2, 4, B, B), F32),
+            pltpu.VMEM((2, B, B), F32),
             pltpu.VMEM((B, B), F32),
             pltpu.VMEM((8, B, B), BF16),
             pltpu.VMEM((8, B, B), BF16),
             pltpu.VMEM((2, 2 * B, B), BF16),
             pltpu.VMEM((2, 2 * B, B), BF16),
             pltpu.VMEM((B, B), F32),
-            dma((5 * PARTS, 3)),
-            dma((5 * PARTS,)),
+            dma((4 * PARTS, 3)),
+            dma((4 * PARTS,)),
             dma((4,)),
             dma((4,)),
             dma((2, PARTS, 3)),
             dma((2, PARTS)),
-            dma((2,)),
+            dma((4,)),
+            dma((4,)),
+            dma((2, PARTS, 3)),
+            dma((2, PARTS)),
             dma((PARTS,)),
             dma((PARTS,)),
         ],

time: 153 us -> 130 us (0.85)
  the two profiles are of different devices: /device:TPU:21 before, /device:TPU:107 now
where the time goes in v5:
time: 130 us
  Pallas kernels  124 us (95%)
  local copies, waits for them, and re-layouts  5.89 us (5%)
    pallas_call x1, Pallas kernels, eliminate(): pl.pallas_call(eliminate_kernel, out_shape=jax.ShapeDtypeStruct((2, B, B)...  108 us
    pallas_call x1, Pallas kernels, gather_heads(): pl.pallas_call(gather_heads_kernel, out_shape=jax.ShapeDtypeStruct((64, L...  7.94 us
    pallas_call x1, Pallas kernels, add_weirs(): pl.pallas_call(weirs_kernel, out_shape=jax.ShapeDtypeStruct((2, B, B), F3...  7.57 us
    unnamed x1, local copies, waits for them, and re-layouts  3.08 us

profile of v5, /device:TPU:107, one launch (start us, length us, event | category | flops | bytes accessed | tf_op | source)
XLA Modules:
  0.0 129.6 jit_solution(1935954307385104546)
XLA Ops:
  0.0 7.9 %gather_heads.1.heads_ref = f32[64,128]{1,0:T(8,128)} custom-call(f32[8,128]{1,0:T(8,128)} %bitcast.13), custom_call_target="tpu_custom_call" | custom-call | tf_op jit(solution)/shard_map/gather_heads/pallas_call | solution.py:73
  7.9 1.4 %pad_bitcast_fusion.2.coef_ref = f32[72,128]{1,0:T(8,128)} fusion(f32[9000]{0:T(1024)} %param.9), kind=kLoop, calls=%fused_computation.2 | loop fusion | bytes 72864 | tf_op jit(solution)/shard_map/reshape | solution.py:188
  9.3 1.4 %pad_bitcast_fusion = (s32[72,128]{1,0:T(8,128)}, s32[72,128]{1,0:T(8,128)}) fusion(s32[9000]{0:T(1024)} %param.11, s32[9000]{0:T(1024)} %param.10), kind=kLoop, calls=%fused_computation | loop fusion | bytes 145728 | tf_op jit(solution)/shard_map/reshape | solution.py:190
  10.8 7.6 %add_weirs.1.a_ref = f32[2,512,512]{2,1,0:T(8,128)} custom-call(s32[16,16]{1,0:T(8,128)} %mask_ref.1, f32[2,512,512]{2,1,0:T(8,128)} %bitcast.12, f32[64,128]{1,0:T(8,128)} %gather_heads.1.heads_ref, f32[72,128]{1,0:T(8,128)} %pad_bitcast_fusion.2.coef_ref, s32[72,128]{1,0:T(8,128)} %get-tuple-element.6.node_ref, s32[72,128]{1,0:T(8,128)} %get-tuple-element.5.cell_ref), custom_call_target="tpu_custom_call" | custom-call | tf_op jit(solution)/shard_map/add_weirs/pallas_call | solution.py:192
  18.3 108.2 %eliminate.1 = f32[2,512,512]{2,1,0:T(8,128)} custom-call(f32[2,512,512]{2,1,0:T(8,128)} %add_weirs.1.a_ref), custom_call_target="tpu_custom_call" | custom-call | tf_op jit(solution)/shard_map/eliminate/pallas_call | solution.py:712
  126.5 3.1 %copy.9 = f32[1,1,2,1,512,512]{5,4,3,2,1,0:T(8,128)} copy(f32[1,1,2,1,512,512]{5,4,3,2,1,0:T(8,128)} %bitcast.11) | data formatting | bytes 4194304

commit v6 on v5

--- a/solution.py
+++ b/solution.py
@@ -220,8 +220,8 @@
     side_recv,
     direct_send,
     direct_recv,
-    inverse_send,
-    inverse_recv,
+    through_send,
+    through_recv,
     last_send,
     last_recv,
 ):
@@ -352,8 +352,6 @@
     side_ways = [
         [[pick(values, place) for values in tree] for tree in TREE_WAYS] for place in places
     ]
-    side_depth[1][1] = jnp.where(r == 0, side_depth[1][2], side_depth[1][1])
-    side_ways[1][1] = [jnp.where(r == 0, v2, v1) for v1, v2 in zip(side_ways[1][1], side_ways[1][2])]
 
     def side_each(s, tree, j, act):
         for way, target in enumerate((ahead, behind, over)):
@@ -362,8 +360,8 @@
             def _():
                 act(side_copy(s, j, way, target))
 
-    def side_slot(slot, panels):
-        for s in panels:
+    def side_slot(slot):
+        for s in range(2):
             for tree in range(3):
                 j = 3 * (slot - 3 * s - SLOTS * side_depth[s][tree]) + tree
 
@@ -377,46 +375,55 @@
 
     SIDE_END = 6 + 4 * SLOTS
 
-    def inverse_copy(b, j, way, target):
-        chunk = panel.at[0, b, pl.ds(pl.multiple_of(j * CHUNK, CHUNK), CHUNK)]
+    def through_copy(b, j, way, target):
+        chunk = panel.at[core, b, pl.ds(pl.multiple_of(j * CHUNK, CHUNK), CHUNK)]
         return pltpu.make_async_remote_copy(
             src_ref=chunk,
             dst_ref=chunk,
-            send_sem=inverse_send.at[b - 2, j, way],
-            recv_sem=inverse_recv.at[b - 2, j],
+            send_sem=through_send.at[b - 2, j, way],
+            recv_sem=through_recv.at[b - 2, j],
             device_id=target,
             device_id_type=MESH,
         )
 
-    def inverse_each(b, tree, j, act):
+    def through_each(b, s, tree, j, act):
         for way, target in enumerate((ahead, behind, over)):
 
-            @pl.when(side_ways[0][tree][way] == 1)
-            def _():
-                act(inverse_copy(b, j, way, target))
-
-    def inverse_slot(b, slot):
+            @pl.when(side_ways[s][tree][way] == 1)
+            def _():
+                act(through_copy(b, j, way, target))
+
+    def through_slot(b, s, slot):
         for tree in range(3):
-            j = 3 * (slot - SLOTS * side_depth[0][tree]) + tree
+            j = 3 * (slot - SLOTS * side_depth[s][tree]) + tree
 
             @pl.when((j >= 0) & (j < PARTS))
             def _():
-                @pl.when(c != 0)
+                @pl.when(c != s)
                 def _():
-                    inverse_copy(b, j, 0, ahead).wait_recv()
-
-                inverse_each(b, tree, j, start)
+                    through_copy(b, j, 0, ahead).wait_recv()
+
+                through_each(b, s, tree, j, start)
                 for kind in range(3):
 
                     @pl.when(lax.rem(b * PARTS + j, 3) == kind)
                     def _():
                         wide_each(kind, b * PARTS + j, start)
 
-    INVERSE_LATER = 4
-    INVERSE_END = (PARTS + 2) // 3 + 4 * SLOTS
-
-    def inverse_pass(b):
-        loop(0, INVERSE_END, lambda slot: inverse_slot(b, slot))
+    THROUGH_END = (PARTS + 2) // 3 + 4 * SLOTS
+
+    def through(b):
+        loop(0, THROUGH_END, lambda slot: through_slot(b, 0, slot))
+
+    def through_sent(b, s):
+        def one(j):
+            for tree in range(3):
+
+                @pl.when(lax.rem(j, 3) == tree)
+                def _():
+                    through_each(b, s, tree, j, sent)
+
+        loop(0, PARTS, one)
 
     def put(index, value):
         high, low = split(value)
@@ -472,26 +479,10 @@
             device_id_type=MESH,
         )
 
-    first_copy = direct_copy(side.at[1], direct.at[0], 0, behind)
+    first_copy = direct_copy(a_ref.at[0], direct.at[0], 0, behind)
     second_copy = direct_copy(direct.at[1], direct.at[1], 1, behind)
-    corner_copy = direct_copy(side.at[1], direct.at[1], 2, pair)
-    cross_copy = direct_copy(side.at[1], panel.at[1, 3], 3, pair)
-    cross_first = direct_copy(direct.at[0], panel.at[1, 3], 3, pair)
-
-    for s in range(2):
-
-        @pl.when(c == s)
-        def _():
-            side[s] = a_ref[0]
-
-    @pl.when(r < 2)
-    def _():
-        panel[core, 0] = a_ref[0]
-        panel[core, 1] = a_ref[1]
-        wide_source(0, start)
-        wide_source(1, start)
-        pair_copy(0).start()
-        pair_copy(1).start()
+    corner_copy = direct_copy(a_ref.at[0], direct.at[1], 2, pair)
+    cross_copy = direct_copy(a_ref.at[0], panel.at[1, 3], 3, pair)
 
     @pl.when((r == 1) & (c == 1))
     def _():
@@ -499,20 +490,38 @@
 
     @pl.when((r == 0) & (c == 1))
     def _():
+        cross_copy.start()
         first_copy.start()
         corner_copy.wait_recv()
         second_copy.start()
 
+    @pl.when((r == 1) & (c == 0))
+    def _():
+        panel[1, 2] = a_ref[0]
+        pair_copy(2).start()
+
+    @pl.when(r < 2)
+    def _():
+        panel[core, 0] = a_ref[0]
+        panel[core, 1] = a_ref[1]
+
+        @pl.when(r == 0)
+        def _():
+            pair_copy(0).start()
+            pair_copy(1).start()
+
+        wide_source(0, start)
+        wide_source(1, start)
+
     @pl.when((r == 0) & (c == 0))
     def _():
-        pivot[...] = side[0]
+        pivot[...] = a_ref[0]
         first = invert()
         panel[0, 2] = first
-        inverse_pass(2)
+        through(2)
         pair_copy(2).start()
         put(0, first)
         first_copy.wait_recv()
-        cross_first.start()
         put(1, direct[0])
         put(2, times(0, 1))
         pair_wait(2)
@@ -520,26 +529,15 @@
         second_copy.wait_recv()
         pivot[...] = direct[1] - times(3, 2)
         panel[0, 3] = invert()
-        inverse_pass(3)
+        through(3)
         loop(0, PARTS, lambda j: last_copy(j).start())
-        loop(0, SIDE_END, lambda slot: side_slot(slot, (1,)))
 
     @pl.when((r == 0) & (c != 0))
     def _():
-        def both(slot):
-            side_slot(slot, (1,))
-
-            @pl.when(slot == SIDE_END - 1)
-            def _():
-                cross_copy.start()
-
-            inverse_slot(2, slot - INVERSE_LATER)
-
-        loop(0, INVERSE_END + INVERSE_LATER, both)
+        through(2)
         pair_copy(2).start()
-        inverse_pass(3)
+        through(3)
         loop(0, PARTS, lambda j: last_copy(j).start())
-        pair_wait(2)
 
     @pl.when(r == 0)
     def _():
@@ -547,38 +545,36 @@
         for j in range(2):
             put(1, a_ref[j])
             out_ref[j] = times(0, 1)
-        pair_wait(0)
-        pair_wait(1)
-        pair_wait(3)
 
     @pl.when(r == 1)
     def _():
-        @pl.when(c == 0)
-        def _():
-            panel[1, 2] = side[0]
-            pair_copy(2).start()
-
-        loop(0, SIDE_END, lambda slot: side_slot(slot, (0,)))
-
-        @pl.when(c != 0)
-        def _():
-            panel[1, 2] = side[0]
-            pair_copy(2).start()
-
-        wide_source(2, start)
-        cross_copy.wait_recv()
-        wide_source(3, start)
-        pair_copy(3).start()
+        @pl.when(c == 1)
+        def _():
+            cross_copy.wait_recv()
+
+        def both(slot):
+            through_slot(2, 0, slot)
+            through_slot(3, 1, slot - 1)
+
+        loop(0, THROUGH_END + 1, both)
+        put(3, panel[1, 2])
 
     @pl.when(r >= 2)
     def _():
+        for s in range(2):
+
+            @pl.when(c == s)
+            def _():
+                side[s] = a_ref[0]
+
         def early(slot):
-            side_slot(slot, (0, 1))
+            side_slot(slot)
             wide_slot(0, 2 * PARTS, slot)
 
         loop(0, SIDE_END, early)
         pair_copy(0).start()
         pair_copy(1).start()
+        put(3, side[0])
 
     @pl.when((r >= 2) & (core == 0))
     def _():
@@ -601,7 +597,6 @@
     @pl.when(r >= 1)
     def _():
         put(0, panel[0, 2])
-        put(3, side[0])
         for j in range(2):
             put(1, panel[0, j])
             put(4 + j, times(0, 1))
@@ -635,6 +630,11 @@
             loop(0, PARTS, lambda j: last_copy(j).wait_recv())
 
         put(0, panel[0, 3])
+
+        @pl.when(r >= 2)
+        def _():
+            put(0, times(4, 0))
+
         for j in range(2):
             scaled = times(0, 6 + j)
             live = c >= 2 if j == 0 else c >= 0
@@ -645,65 +645,64 @@
 
             @pl.when((r >= 2) & live)
             def _():
-                put(5, scaled)
-                out_ref[j] = out_ref[j] - times(4, 5)
+                out_ref[j] = out_ref[j] - scaled
 
     @pl.when(c == 0)
     def _():
         out_ref[0] = a_ref[0]
 
-    def side_sent(s):
-        def one(j):
-            for tree in range(3):
-
-                @pl.when(lax.rem(j, 3) == tree)
-                def _():
-                    side_each(s, tree, j, sent)
-
-        loop(0, PARTS, one)
-
-    @pl.when(r >= 1)
-    def _():
-        side_sent(0)
-
-    @pl.when(r != 1)
-    def _():
-        side_sent(1)
+    for b in range(4):
+        wide_source(b, sent)
+
+    @pl.when(r < 2)
+    def _():
+        through_sent(2, 0)
 
     @pl.when(r == 0)
     def _():
-        def one(j):
-            for tree in range(3):
-
-                @pl.when(lax.rem(j, 3) == tree)
-                def _():
-                    inverse_each(2, tree, j, sent)
-                    inverse_each(3, tree, j, sent)
-
-        loop(0, PARTS, one)
-        cross_copy.wait_send()
+        through_sent(3, 0)
 
         @pl.when(c == 1)
         def _():
+            cross_copy.wait_send()
             first_copy.wait_send()
             second_copy.wait_send()
 
-    for b in range(4):
-        wide_source(b, sent)
-    for b in range(3):
-        pair_copy(b).wait_send()
+    @pl.when(r == 1)
+    def _():
+        through_sent(3, 1)
+
+        @pl.when(c == 0)
+        def _():
+            pair_copy(2).wait_send()
+
+        @pl.when(c == 1)
+        def _():
+            corner_copy.wait_send()
 
     @pl.when(core == 0)
     def _():
+        for b in range(3):
+            pair_copy(b).wait_send()
         loop(0, PARTS, lambda j: last_copy(j).wait_send())
 
-    @pl.when(core == 1)
-    def _():
-        pair_copy(3).wait_send()
-
-    @pl.when((r == 1) & (c == 1))
-    def _():
-        corner_copy.wait_send()
+    @pl.when(r >= 2)
+    def _():
+        @pl.when(core == 1)
+        def _():
+            for b in range(4):
+                pair_copy(b).wait_send()
+
+        for s in range(2):
+
+            def one(j):
+                for tree in range(3):
+
+                    @pl.when(lax.rem(j, 3) == tree)
+                    def _():
+                        side_each(s, tree, j, sent)
+
+            loop(0, PARTS, one)
 
 
 def eliminate(blocks):

time: 130 us -> 122 us (0.938)
  the two profiles are of different devices: /device:TPU:107 before, /device:TPU:21 now
where the time goes in v6:
time: 122 us; the launch traced here: 121 us
  Pallas kernels  115 us (94%)
  local copies, waits for them, and re-layouts  5.89 us (5%)
    pallas_call x1, Pallas kernels, eliminate(): pl.pallas_call(eliminate_kernel, out_shape=jax.ShapeDtypeStruct((2, B, B)...  98.8 us
    pallas_call x1, Pallas kernels, gather_heads(): pl.pallas_call(gather_heads_kernel, out_shape=jax.ShapeDtypeStruct((64, L...  9.79 us
    pallas_call x1, Pallas kernels, add_weirs(): pl.pallas_call(weirs_kernel, out_shape=jax.ShapeDtypeStruct((2, B, B), F3...  6.67 us
    unnamed x1, local copies, waits for them, and re-layouts  3.08 us

profile of v6, /device:TPU:21, one launch (start us, length us, event | category | flops | bytes accessed | tf_op | source)
XLA Modules:
  0.0 121.2 jit_solution(10313467040156672129)
XLA Ops:
  0.0 9.8 %gather_heads.1.heads_ref = f32[64,128]{1,0:T(8,128)} custom-call(f32[8,128]{1,0:T(8,128)} %bitcast.13), custom_call_target="tpu_custom_call" | custom-call | tf_op jit(solution)/shard_map/gather_heads/pallas_call | solution.py:73
  9.8 1.4 %pad_bitcast_fusion.2.coef_ref = f32[72,128]{1,0:T(8,128)} fusion(f32[9000]{0:T(1024)} %param.9), kind=kLoop, calls=%fused_computation.2 | loop fusion | bytes 72864 | tf_op jit(solution)/shard_map/reshape | solution.py:188
  11.2 1.4 %pad_bitcast_fusion = (s32[72,128]{1,0:T(8,128)}, s32[72,128]{1,0:T(8,128)}) fusion(s32[9000]{0:T(1024)} %param.11, s32[9000]{0:T(1024)} %param.10), kind=kLoop, calls=%fused_computation | loop fusion | bytes 145728 | tf_op jit(solution)/shard_map/reshape | solution.py:190
  12.6 6.7 %add_weirs.1.a_ref = f32[2,512,512]{2,1,0:T(8,128)} custom-call(s32[16,16]{1,0:T(8,128)} %mask_ref.1, f32[2,512,512]{2,1,0:T(8,128)} %bitcast.12, f32[64,128]{1,0:T(8,128)} %gather_heads.1.heads_ref, f32[72,128]{1,0:T(8,128)} %pad_bitcast_fusion.2.coef_ref, s32[72,128]{1,0:T(8,128)} %get-tuple-element.6.node_ref, s32[72,128]{1,0:T(8,128)} %get-tuple-element.5.cell_ref), custom_call_target="tpu_custom_call" | custom-call | tf_op jit(solution)/shard_map/add_weirs/pallas_call | solution.py:192
  19.3 98.8 %eliminate.1 = f32[2,512,512]{2,1,0:T(8,128)} custom-call(f32[2,512,512]{2,1,0:T(8,128)} %add_weirs.1.a_ref), custom_call_target="tpu_custom_call" | custom-call | tf_op jit(solution)/shard_map/eliminate/pallas_call | solution.py:711
  118.1 3.1 %copy.9 = f32[1,1,2,1,512,512]{5,4,3,2,1,0:T(8,128)} copy(f32[1,1,2,1,512,512]{5,4,3,2,1,0:T(8,128)} %bitcast.11) | data formatting | bytes 4194304

commit v7 on v6

--- a/solution.py
+++ b/solution.py
@@ -43,44 +43,6 @@
     return dot(ah, bh) + dot(ah, bl) + dot(al, bh)
 
 
-def gather_heads_kernel(mine_ref, every_ref, send_sem, recv_sem):
-    r = lax.axis_index("wide")
-    c = lax.axis_index("narrow")
-    count = 8
-    barrier = pltpu.get_barrier_semaphore()
-    for hop in range(1, count):
-        pl.semaphore_signal(barrier, inc=1, device_id=(r, lax.rem(c + hop, count)), device_id_type=MESH)
-    pl.semaphore_wait(barrier, count - 1)
-    place = pl.ds(pl.multiple_of(c * 8, 8), 8)
-    copies = []
-    for hop in range(1, count):
-        copy = pltpu.make_async_remote_copy(
-            src_ref=mine_ref,
-            dst_ref=every_ref.at[place],
-            send_sem=send_sem.at[hop],
-            recv_sem=recv_sem.at[hop],
-            device_id=(r, lax.rem(c + hop, count)),
-            device_id_type=MESH,
-        )
-        copy.start()
-        copies.append(copy)
-    every_ref[place] = mine_ref[...]
-    for copy in copies:
-        copy.wait()
-
-
-def gather_heads(heads):
-    return pl.pallas_call(
-        gather_heads_kernel,
-        out_shape=jax.ShapeDtypeStruct((64, LANES), F32),
-        in_specs=[pl.BlockSpec(memory_space=pltpu.VMEM)],
-        out_specs=pl.BlockSpec(memory_space=pltpu.VMEM),
-        scratch_shapes=[pltpu.SemaphoreType.DMA((8,)), pltpu.SemaphoreType.DMA((8,))],
-        compiler_params=pltpu.CompilerParams(collective_id=0, has_side_effects=True),
-        name="gather_heads",
-    )(heads.reshape(8, LANES))
-
-
 def lookup(table_ref, first, index):
     high = lax.shift_right_logical(index, 7) - first
     low = jnp.bitwise_and(index, 127)
@@ -99,110 +61,21 @@
     return high, middle, rest - middle
 
 
-def weirs_kernel(mask_ref, base_ref, heads_ref, coef_ref, node_ref, cell_ref, out_ref, code_ref, flux_ref):
-    r = lax.axis_index("wide")
-    c = lax.axis_index("narrow")
-    upper = r < 8
-    for j in range(2):
-        col = c + 8 * j
-        keep = jnp.where((mask_ref[r, col] != 0) | (r == col), 1.0, 0.0).astype(F32)
-        out_ref[j] = base_ref[j] * keep
-    node = node_ref[...]
-    cell = cell_ref[...]
-    drop = lookup(heads_ref, 0, node) - lookup(heads_ref, 32, cell)
-    flux = 1.5 * coef_ref[...] * jnp.sqrt(drop * drop + 0.01)
-    row = jnp.where(upper, node, cell)
-    col = jnp.where(upper, cell, node)
-    mine = lax.shift_right_logical(row, 9) == r
-    low_row = jnp.bitwise_and(row, 511)
-
-    target = jnp.where(upper, c + 8, c)
-    slot = jnp.where(upper, 1, 0)
-    hit = jnp.where(mine & (lax.shift_right_logical(col, 9) == target), 1, 0)
-    code = low_row * 512 + jnp.bitwise_and(col, 511)
-    steps = jnp.max(jnp.sum(hit.astype(F32), axis=0, keepdims=True)).astype(jnp.int32)
-    code_ref[...] = jnp.zeros(code_ref.shape, jnp.int32)
-    flux_ref[...] = jnp.zeros(flux_ref.shape, F32)
-    place = lax.broadcasted_iota(jnp.int32, (ROWS, LANES), 0)
-
-    def extract(s, left):
-        first = jnp.min(jnp.where(left != 0, place, ROWS), axis=0, keepdims=True)
-        now = place == first
-        code_ref[pl.ds(s, 1), :] = jnp.sum(jnp.where(now, code, 0), axis=0, keepdims=True)
-        flux_ref[pl.ds(s, 1), :] = jnp.sum(jnp.where(now, flux, 0.0), axis=0, keepdims=True)
-        return jnp.where(now, 0, left)
-
-    lax.fori_loop(0, steps, extract, hit)
-
-    def scatter(b, carry):
-        rows = pl.ds(pl.multiple_of(b * 8, 8), 8)
-        codes = code_ref[rows]
-        parts = pieces(flux_ref[rows])
-        here = lax.broadcasted_iota(jnp.int32, (B, LANES), 0)
-        row_of = lax.shift_right_logical(codes, 9)
-        col_of = jnp.bitwise_and(codes, 511)
-        right = jnp.concatenate(
-            [jnp.where(here == col_of[s : s + 1], 1.0, 0.0).astype(BF16) for s in range(8)], axis=1
-        )
-        total = jnp.zeros((B, B), F32)
-        for part in parts:
-            left = jnp.concatenate(
-                [jnp.where(here == row_of[s : s + 1], part[s : s + 1], 0.0).astype(BF16) for s in range(8)],
-                axis=1,
-            )
-            total = total + dot_nt(left, right)
-        out_ref[slot] = out_ref[slot] - total
-        return carry
-
-    lax.fori_loop(0, lax.div(steps + 7, 8), scatter, 0)
-
-    @pl.when(c == lax.rem(r, 8))
-    def _():
-        own = jnp.where(mine, flux, 0.0)
-        parts = pieces(own)
-        high = lax.shift_right_logical(low_row, 7)
-        low = jnp.bitwise_and(low_row, 127)
-        here8 = lax.broadcasted_iota(jnp.int32, (8, LANES), 0)
-        here128 = lax.broadcasted_iota(jnp.int32, (LANES, LANES), 0)
-        total = jnp.zeros((24, LANES), F32)
-        for g in range(ROWS // 8):
-            ones = []
-            lefts = []
-            for s in range(8 * g, 8 * g + 8):
-                ones.append(jnp.where(here128 == low[s : s + 1], 1.0, 0.0).astype(BF16))
-                at = here8 == high[s : s + 1]
-                lefts.append(
-                    jnp.concatenate([jnp.where(at, part[s : s + 1], 0.0) for part in parts], axis=0).astype(BF16)
-                )
-            total = total + dot_nt(jnp.concatenate(lefts, axis=1), jnp.concatenate(ones, axis=1))
-        diagonal = total[0:8] + total[8:16] + total[16:24]
-        eye = here128 == lax.broadcasted_iota(jnp.int32, (LANES, LANES), 1)
-        which = jnp.where(upper, 0, 1)
-        for t in range(4):
-            part = pl.ds(t * LANES, LANES)
-            out_ref[which, part, part] = out_ref[which, part, part] + jnp.where(eye, diagonal[t : t + 1], 0.0)
-
-
-def add_weirs(base, block_mask, every_head, coef, weir_node, weir_cell):
-    pad = ROWS * LANES - coef.shape[0]
-    coef = jnp.pad(coef, (0, pad)).reshape(ROWS, LANES)
-    node = jnp.pad(weir_node, (0, pad)).reshape(ROWS, LANES)
-    cell = jnp.pad(weir_cell, (0, pad), constant_values=4096).reshape(ROWS, LANES)
-    vmem = pl.BlockSpec(memory_space=pltpu.VMEM)
-    return pl.pallas_call(
-        weirs_kernel,
-        out_shape=jax.ShapeDtypeStruct((2, B, B), F32),
-        in_specs=[pl.BlockSpec(memory_space=pltpu.SMEM)] + [vmem] * 5,
-        out_specs=vmem,
-        scratch_shapes=[pltpu.VMEM((ROWS, LANES), jnp.int32), pltpu.VMEM((ROWS, LANES), F32)],
-        compiler_params=pltpu.CompilerParams(vmem_limit_bytes=VMEM_LIMIT),
-        name="add_weirs",
-    )(block_mask, base, every_head, coef, node, cell)
-
-
-def eliminate_kernel(
-    a_ref,
+def solve_kernel(
+    mask_ref,
+    base_ref,
+    heads_ref,
+    coef_ref,
+    node_ref,
+    cell_ref,
     out_ref,
+    own,
+    every,
+    row_of,
+    col_of,
+    flux_high,
+    flux_low,
+    diagonal,
     side,
     panel,
     direct,
@@ -224,6 +97,8 @@
     through_recv,
     last_send,
     last_recv,
+    heads_send,
+    heads_recv,
 ):
     r = lax.axis_index("wide")
     c = lax.axis_index("narrow")
@@ -242,9 +117,11 @@
     over = (r, (1 - far) * 4 + z)
 
     barrier = pltpu.get_barrier_semaphore()
-    for peer in (up, down, across, pair, ahead, behind, over):
+    for peer in (up, down, across, pair):
         pl.semaphore_signal(barrier, inc=1, device_id=peer, device_id_type=MESH)
-    pl.semaphore_wait(barrier, 7)
+    for hop in range(1, 8):
+        pl.semaphore_signal(barrier, inc=1, device_id=(r, lax.rem(c + hop, 8)), device_id_type=MESH)
+    pl.semaphore_wait(barrier, 11)
 
     def loop(first, last, act):
         lax.fori_loop(first, last, lambda i, carry: (act(i), carry)[1], 0)
@@ -479,54 +356,158 @@
             device_id_type=MESH,
         )
 
-    first_copy = direct_copy(a_ref.at[0], direct.at[0], 0, behind)
+    raw = panel.at[core, 0]
+    first_copy = direct_copy(raw, direct.at[0], 0, behind)
     second_copy = direct_copy(direct.at[1], direct.at[1], 1, behind)
-    corner_copy = direct_copy(a_ref.at[0], direct.at[1], 2, pair)
-    cross_copy = direct_copy(a_ref.at[0], panel.at[1, 3], 3, pair)
-
-    @pl.when((r == 1) & (c == 1))
-    def _():
-        corner_copy.start()
+    corner_copy = direct_copy(raw, direct.at[1], 2, pair)
+    cross_copy = direct_copy(raw, panel.at[1, 3], 3, pair)
+
+    def heads_copy(hop):
+        return pltpu.make_async_remote_copy(
+            src_ref=heads_ref,
+            dst_ref=every.at[pl.ds(pl.multiple_of(c * 8, 8), 8)],
+            send_sem=heads_send.at[hop],
+            recv_sem=heads_recv.at[hop],
+            device_id=(r, lax.rem(c + hop, 8)),
+            device_id_type=MESH,
+        )
+
+    loop(1, 8, lambda hop: heads_copy(hop).start())
+    every[pl.ds(pl.multiple_of(c * 8, 8), 8)] = heads_ref[...]
+
+    for j in range(2):
+        col = c + 8 * j
+        keep = jnp.where((mask_ref[r, col] != 0) | (r == col), 1.0, 0.0).astype(F32)
+        own[j] = base_ref[j] * keep
+
+    @pl.when(r < 2)
+    def _():
+        panel[core, 0] = own[0]
+
+        @pl.when((r == 1) & (c == 1))
+        def _():
+            corner_copy.start()
+
+        @pl.when((r == 0) & (c == 1))
+        def _():
+            cross_copy.start()
+            first_copy.start()
+
+        @pl.when((r == 1) & (c == 0))
+        def _():
+            panel[1, 2] = own[0]
+            pair_copy(2).start()
+
+        @pl.when(r == 0)
+        def _():
+            pair_copy(0).start()
+
+        wide_source(0, start)
+
+    for s in range(2):
+
+        @pl.when((r >= 2) & (r < 8) & (c == s))
+        def _():
+            side[s] = own[0]
+
+    loop(1, 8, lambda hop: heads_copy(hop).wait_recv())
+    upper = r < 8
+    node = node_ref[...]
+    cell = cell_ref[...]
+    drop = lookup(every, 0, node) - lookup(every, 32, cell)
+    flux = 1.5 * coef_ref[...] * jnp.sqrt(drop * drop + 0.01)
+    weir_row = jnp.where(upper, node, cell)
+    weir_col = jnp.where(upper, cell, node)
+    hit = (lax.shift_right_logical(weir_row, 9) == r) & (
+        lax.shift_right_logical(weir_col, 9) == jnp.where(upper, c + 8, c)
+    )
+    row_of[...] = jnp.bitwise_and(weir_row, 511)
+    col_of[...] = jnp.bitwise_and(weir_col, 511)
+    high, middle, low = pieces(flux)
+    flux_high[...] = jnp.where(hit, high, 0.0)
+    flux_low[...] = jnp.where(hit, flux - high, 0.0)
+    slot_of = jnp.where(upper, 1, 0)
+
+    def add_diagonal(ref, at, first):
+        here = lax.broadcasted_iota(jnp.int32, (LANES, LANES), 0)
+        eye = here == lax.broadcasted_iota(jnp.int32, (LANES, LANES), 1)
+        for t in range(4):
+            part = pl.ds(t * LANES, LANES)
+            ref[at, part, part] = ref[at, part, part] + jnp.where(eye, diagonal[first + t : first + t + 1], 0.0)
+
+    @pl.when(c == lax.rem(r, 8))
+    def _():
+        strip = lax.shift_right_logical(weir_row, 7) - 4 * r
+        lane = jnp.bitwise_and(weir_row, 127)
+        here8 = lax.broadcasted_iota(jnp.int32, (8, LANES), 0)
+        here128 = lax.broadcasted_iota(jnp.int32, (LANES, LANES), 0)
+        total = jnp.zeros((24, LANES), F32)
+        for g in range(ROWS // 8):
+            ones = []
+            lefts = []
+            for t in range(8 * g, 8 * g + 8):
+                ones.append(jnp.where(here128 == lane[t : t + 1], 1.0, 0.0).astype(BF16))
+                at = here8 == strip[t : t + 1]
+                lefts.append(
+                    jnp.concatenate(
+                        [jnp.where(at, part[t : t + 1], 0.0) for part in (high, middle, low)], axis=0
+                    ).astype(BF16)
+                )
+            total = total + dot_nt(jnp.concatenate(lefts, axis=1), jnp.concatenate(ones, axis=1))
+        diagonal[...] = total[0:8] + total[8:16] + total[16:24]
+        add_diagonal(own, jnp.where(upper, 0, 1), 0)
+
+    def scatter(b):
+        rows = pl.ds(pl.multiple_of(b * 8, 8), 8)
+        here = lax.broadcasted_iota(jnp.int32, (B, LANES), 0)
+        at_row = row_of[rows]
+        at_col = col_of[rows]
+        right = jnp.concatenate(
+            [jnp.where(here == at_col[t : t + 1], 1.0, 0.0).astype(BF16) for t in range(8)], axis=1
+        )
+        total = jnp.zeros((B, B), F32)
+        for part in (flux_high[rows], flux_low[rows]):
+            left = jnp.concatenate(
+                [jnp.where(here == at_row[t : t + 1], part[t : t + 1], 0.0).astype(BF16) for t in range(8)],
+                axis=1,
+            )
+            total = total + dot_nt(left, right)
+        own[slot_of] = own[slot_of] - total
+
+    STEPS = ROWS // 8
+    LATER = (STEPS + 1) // 2
+
+    def second_block():
+        panel[core, 1] = own[1]
+
+        @pl.when(r == 0)
+        def _():
+            pair_copy(1).start()
+
+        wide_source(1, start)
 
     @pl.when((r == 0) & (c == 1))
     def _():
-        cross_copy.start()
-        first_copy.start()
         corner_copy.wait_recv()
         second_copy.start()
 
-    @pl.when((r == 1) & (c == 0))
-    def _():
-        panel[1, 2] = a_ref[0]
-        pair_copy(2).start()
-
-    @pl.when(r < 2)
-    def _():
-        panel[core, 0] = a_ref[0]
-        panel[core, 1] = a_ref[1]
-
-        @pl.when(r == 0)
-        def _():
-            pair_copy(0).start()
-            pair_copy(1).start()
-
-        wide_source(0, start)
-        wide_source(1, start)
-
     @pl.when((r == 0) & (c == 0))
     def _():
-        pivot[...] = a_ref[0]
+        pivot[...] = own[0]
         first = invert()
         panel[0, 2] = first
         through(2)
         pair_copy(2).start()
         put(0, first)
+        loop(0, STEPS, scatter)
+        second_block()
         first_copy.wait_recv()
         put(1, direct[0])
         put(2, times(0, 1))
         pair_wait(2)
         put(3, panel[1, 2])
         second_copy.wait_recv()
+        add_diagonal(direct, 1, 4)
         pivot[...] = direct[1] - times(3, 2)
         panel[0, 3] = invert()
         through(3)
@@ -534,6 +515,8 @@
 
     @pl.when((r == 0) & (c != 0))
     def _():
+        loop(0, STEPS, scatter)
+        second_block()
         through(2)
         pair_copy(2).start()
         through(3)
@@ -543,7 +526,7 @@
     def _():
         put(0, panel[0, 2])
         for j in range(2):
-            put(1, a_ref[j])
+            put(1, own[j])
             out_ref[j] = times(0, 1)
 
     @pl.when(r == 1)
@@ -554,76 +537,119 @@
 
         def both(slot):
             through_slot(2, 0, slot)
-            through_slot(3, 1, slot - 1)
-
-        loop(0, THROUGH_END + 1, both)
+            through_slot(3, 1, slot - 3)
+
+        loop(0, STEPS, scatter)
+        second_block()
+        loop(0, THROUGH_END + 3, both)
         put(3, panel[1, 2])
 
     @pl.when(r >= 2)
     def _():
+        end = jnp.where(core == 0, 3 * PARTS, 4 * PARTS)
+        behind_by = jnp.where(upper, 0, LATER)
+
+        def early(slot):
+            wide_slot(0, end, slot)
+            side_slot(slot - behind_by)
+            for b in range(3):
+
+                @pl.when(slot == (b * PARTS + PARTS - 1) // 3 + 4 * SLOTS)
+                def _():
+                    pair_copy(b).start()
+
+        def step(slot):
+            scatter(2 * slot)
+
+            @pl.when(2 * slot + 1 < STEPS)
+            def _():
+                scatter(2 * slot + 1)
+
+            early(slot)
+
+        loop(0, LATER, step)
         for s in range(2):
 
-            @pl.when(c == s)
-            def _():
-                side[s] = a_ref[0]
-
-        def early(slot):
-            side_slot(slot)
-            wide_slot(0, 2 * PARTS, slot)
-
-        loop(0, SIDE_END, early)
-        pair_copy(0).start()
-        pair_copy(1).start()
+            @pl.when((r >= 8) & (c == s))
+            def _():
+                side[s] = own[0]
+
+        loop(LATER, SIDE_END + LATER + 1, early)
+
+        @pl.when(core == 1)
+        def _():
+            pair_copy(3).start()
+
         put(3, side[0])
 
-    @pl.when((r >= 2) & (core == 0))
-    def _():
-        wide_relay(2, 3)
-        pair_copy(2).start()
+        @pl.when(core == 0)
+        def _():
+            for b in range(3):
+                pair_wait(b)
+
+    @pl.when(core == 1)
+    def _():
         for b in range(3):
             pair_wait(b)
 
-    @pl.when((r >= 2) & (core == 1))
-    def _():
-        wide_relay(2, 4)
-        pair_copy(2).start()
-        pair_copy(3).start()
-
-    @pl.when(core == 1)
-    def _():
-        for b in range(3):
-            pair_wait(b)
-
-    @pl.when(r >= 1)
-    def _():
-        put(0, panel[0, 2])
-        for j in range(2):
-            put(1, panel[0, j])
-            put(4 + j, times(0, 1))
-            kept = a_ref[j] - times(3, 4 + j)
-            out_ref[j] = kept
-
-            @pl.when(r == 1)
-            def _():
-                put(6 + j, kept)
-
+    last_first = jnp.where((core == 0) & (r >= 2), 3 * PARTS, 4 * PARTS)
+
+    def last_slot(slot):
+        wide_slot(last_first, 4 * PARTS, slot, forward=True)
+
+    def scaled_row(j):
+        put(1, panel[0, j])
+        put(4 + j, times(0, 1))
+
+    def kept_row(j):
+        kept = own[j] - times(3, 4 + j)
+        out_ref[j] = kept
+
+        @pl.when(r == 1)
+        def _():
+            put(6 + j, kept)
+
+    def first_rest(j):
         @pl.when(r >= 2)
         def _():
-            put(1, panel[1, 2])
-            for j in range(2):
-                put(6 + j, panel[1, j] - times(1, 4 + j))
-
+            if j == 0:
+                put(1, panel[1, 2])
+            put(6 + j, panel[1, j] - times(1, 4 + j))
+
+    def corner_row():
+        @pl.when(r >= 2)
+        def _():
             @pl.when(core == 0)
             def _():
                 pair_wait(3)
 
             put(1, panel[1, 3])
             put(2, times(0, 1))
+
+    def column():
+        @pl.when(r >= 2)
+        def _():
             put(4, side[1] - times(3, 2))
 
-        @pl.when((r >= 2) & (core == 0))
-        def _():
-            wide_relay(3, 4, forward=True)
+    @pl.when(r >= 1)
+    def _():
+        put(0, panel[0, 2])
+        work = [
+            lambda: scaled_row(0),
+            lambda: scaled_row(1),
+            lambda: kept_row(0),
+            lambda: kept_row(1),
+            lambda: first_rest(0),
+            lambda: first_rest(1),
+            corner_row,
+            column,
+        ]
+        base = 3 * PARTS // 3
+        slots = list(range(base, base + 3 + 4 * SLOTS + 1))
+        for k, slot in enumerate(slots):
+            last_slot(slot)
+            if k < len(work):
+                work[k]()
 
         @pl.when(core == 1)
         def _():
@@ -649,8 +675,9 @@
 
     @pl.when(c == 0)
     def _():
-        out_ref[0] = a_ref[0]
-
+        out_ref[0] = own[0]
+
+    loop(1, 8, lambda hop: heads_copy(hop).wait_send())
     for b in range(4):
         wide_source(b, sent)
 
@@ -705,15 +732,27 @@
             loop(0, PARTS, one)
 
 
-def eliminate(blocks):
+def per_device(base, block_mask, heads, coef, weir_node, weir_cell):
+    pad = ROWS * LANES - coef.shape[0]
+    coef = jnp.pad(coef, (0, pad)).reshape(ROWS, LANES)
+    node = jnp.pad(weir_node, (0, pad)).reshape(ROWS, LANES)
+    cell = jnp.pad(weir_cell, (0, pad), constant_values=4096).reshape(ROWS, LANES)
     vmem = pl.BlockSpec(memory_space=pltpu.VMEM)
     dma = pltpu.SemaphoreType.DMA
-    return pl.pallas_call(
-        eliminate_kernel,
+    weirs = (ROWS, LANES)
+    out = pl.pallas_call(
+        solve_kernel,
         out_shape=jax.ShapeDtypeStruct((2, B, B), F32),
-        in_specs=[vmem],
+        in_specs=[pl.BlockSpec(memory_space=pltpu.SMEM)] + [vmem] * 5,
         out_specs=vmem,
         scratch_shapes=[
+            pltpu.VMEM((2, B, B), F32),
+            pltpu.VMEM((64, LANES), F32),
+            pltpu.VMEM(weirs, jnp.int32),
+            pltpu.VMEM(weirs, jnp.int32),
+            pltpu.VMEM(weirs, F32),
+            pltpu.VMEM(weirs, F32),
+            pltpu.VMEM((8, LANES), F32),
             pltpu.VMEM((2, B, B), F32),
             pltpu.VMEM((2, 4, B, B), F32),
             pltpu.VMEM((2, B, B), F32),
@@ -735,19 +774,15 @@
             dma((2, PARTS)),
             dma((PARTS,)),
             dma((PARTS,)),
+            dma((8,)),
+            dma((8,)),
         ],
         compiler_params=pltpu.CompilerParams(
-            collective_id=1, has_side_effects=True, vmem_limit_bytes=VMEM_LIMIT
+            collective_id=0, has_side_effects=True, vmem_limit_bytes=VMEM_LIMIT
         ),
-        name="eliminate",
-    )(blocks)
-
-
-def per_device(base, block_mask, heads, coef, weir_node, weir_cell):
-    blocks = base.reshape(2, B, B)
-    every_head = gather_heads(heads)
-    blocks = add_weirs(blocks, block_mask, every_head, coef, weir_node, weir_cell)
-    return eliminate(blocks).reshape(base.shape)
+        name="solve",
+    )(block_mask, base.reshape(2, B, B), heads.reshape(8, LANES), coef, node, cell)
+    return out.reshape(base.shape)
 
 
 def solution(mesh):

time: 122 us -> 124 us (1.016); the launches traced: 121 us -> 122 us
    pallas_call x3 -> x1, Pallas kernels: 115 us -> 116 us  [per_device(): pl.pallas_call(solve_kernel, out_shape=jax.ShapeDtypeStruct((2, B, B), F3...]
where the time goes in v7:
time: 124 us; the launch traced here: 122 us
  Pallas kernels  116 us (94%)
  local copies, waits for them, and re-layouts  5.88 us (5%)
    pallas_call x1, Pallas kernels, per_device(): pl.pallas_call(solve_kernel, out_shape=jax.ShapeDtypeStruct((2, B, B), F3...  116 us
    unnamed x1, local copies, waits for them, and re-layouts  3.08 us

profile of v7, /device:TPU:21, one launch (start us, length us, event | category | flops | bytes accessed | tf_op | source)
XLA Modules:
  0.0 121.5 jit_solution(10745467495477242217)
XLA Ops:
  0.0 1.4 %pad_bitcast_fusion.2.coef_ref = f32[72,128]{1,0:T(8,128)} fusion(f32[9000]{0:T(1024)} %param.9), kind=kLoop, calls=%fused_computation.2 | loop fusion | bytes 72864 | tf_op jit(solution)/shard_map/reshape | solution.py:737
  1.4 1.4 %pad_bitcast_fusion = (s32[72,128]{1,0:T(8,128)}, s32[72,128]{1,0:T(8,128)}) fusion(s32[9000]{0:T(1024)} %param.11, s32[9000]{0:T(1024)} %param.10), kind=kLoop, calls=%fused_computation | loop fusion | bytes 145728 | tf_op jit(solution)/shard_map/reshape | solution.py:739
  2.8 115.6 %solve.1 = f32[2,512,512]{2,1,0:T(8,128)} custom-call(s32[16,16]{1,0:T(8,128)} %mask_ref.1, f32[2,512,512]{2,1,0:T(8,128)} %bitcast.12, f32[8,128]{1,0:T(8,128)} %bitcast.13, f32[72,128]{1,0:T(8,128)} %pad_bitcast_fusion.2.coef_ref, s32[72,128]{1,0:T(8,128)} %get-tuple-element.6.node_ref, s32[72,128]{1,0:T(8,128)} %get-tuple-element.5.cell_ref), custom_call_target="tpu_custom_call" | custom-call | tf_op jit(solution)/shard_map/solve/pallas_call | solution.py:743
  118.5 3.1 %copy.9 = f32[1,1,2,1,512,512]{5,4,3,2,1,0:T(8,128)} copy(f32[1,1,2,1,512,512]{5,4,3,2,1,0:T(8,128)} %bitcast.11) | data formatting | bytes 4194304

commit v8 on v6

--- a/solution.py
+++ b/solution.py
@@ -594,36 +594,64 @@
         for b in range(3):
             pair_wait(b)
 
-    @pl.when(r >= 1)
-    def _():
-        put(0, panel[0, 2])
-        for j in range(2):
-            put(1, panel[0, j])
-            put(4 + j, times(0, 1))
-            kept = a_ref[j] - times(3, 4 + j)
-            out_ref[j] = kept
-
-            @pl.when(r == 1)
-            def _():
-                put(6 + j, kept)
-
+    last_first = jnp.where((core == 0) & (r >= 2), 3 * PARTS, 4 * PARTS)
+
+    def last_slot(slot):
+        wide_slot(last_first, 4 * PARTS, slot, forward=True)
+
+    def scaled_row(j):
+        put(1, panel[0, j])
+        put(4 + j, times(0, 1))
+
+    def kept_row(j):
+        kept = a_ref[j] - times(3, 4 + j)
+        out_ref[j] = kept
+
+        @pl.when(r == 1)
+        def _():
+            put(6 + j, kept)
+
+    def first_rest(j):
         @pl.when(r >= 2)
         def _():
-            put(1, panel[1, 2])
-            for j in range(2):
-                put(6 + j, panel[1, j] - times(1, 4 + j))
-
+            if j == 0:
+                put(1, panel[1, 2])
+            put(6 + j, panel[1, j] - times(1, 4 + j))
+
+    def corner_row():
+        @pl.when(r >= 2)
+        def _():
             @pl.when(core == 0)
             def _():
                 pair_wait(3)
 
             put(1, panel[1, 3])
             put(2, times(0, 1))
+
+    def column():
+        @pl.when(r >= 2)
+        def _():
             put(4, side[1] - times(3, 2))
 
-        @pl.when((r >= 2) & (core == 0))
-        def _():
-            wide_relay(3, 4, forward=True)
+    @pl.when(r >= 1)
+    def _():
+        put(0, panel[0, 2])
+        work = [
+            lambda: scaled_row(0),
+            lambda: scaled_row(1),
+            lambda: kept_row(0),
+            lambda: kept_row(1),
+            lambda: first_rest(0),
+            lambda: first_rest(1),
+            corner_row,
+            column,
+        ]
+        base = 3 * PARTS // 3
+        slots = list(range(base, base + 3 + 4 * SLOTS + 1))
+        for k, slot in enumerate(slots):
+            last_slot(slot)
+            if k < len(work):
+                work[k]()
 
         @pl.when(core == 1)
         def _():

time: 122 us -> 120 us (0.984)
  Pallas kernels: 115 us -> 112 us
    pallas_call x1, Pallas kernels: 98.8 us -> 95.8 us  [eliminate(): pl.pallas_call(eliminate_kernel, out_shape=jax.ShapeDtypeStruct((2, B, B)...]
where the time goes in v8:
time: 120 us; the launch traced here: 118 us
  Pallas kernels  112 us (93%)
  local copies, waits for them, and re-layouts  5.89 us (5%)
    pallas_call x1, Pallas kernels, eliminate(): pl.pallas_call(eliminate_kernel, out_shape=jax.ShapeDtypeStruct((2, B, B)...  95.8 us
    pallas_call x1, Pallas kernels, gather_heads(): pl.pallas_call(gather_heads_kernel, out_shape=jax.ShapeDtypeStruct((64, L...  9.79 us
    pallas_call x1, Pallas kernels, add_weirs(): pl.pallas_call(weirs_kernel, out_shape=jax.ShapeDtypeStruct((2, B, B), F3...  6.67 us
    unnamed x1, local copies, waits for them, and re-layouts  3.08 us

profile of v8, /device:TPU:21, one launch (start us, length us, event | category | flops | bytes accessed | tf_op | source)
XLA Modules:
  0.0 118.2 jit_solution(2370935592983399884)
XLA Ops:
  0.0 9.8 %gather_heads.1.heads_ref = f32[64,128]{1,0:T(8,128)} custom-call(f32[8,128]{1,0:T(8,128)} %bitcast.13), custom_call_target="tpu_custom_call" | custom-call | tf_op jit(solution)/shard_map/gather_heads/pallas_call | solution.py:73
  9.8 1.4 %pad_bitcast_fusion.2.coef_ref = f32[72,128]{1,0:T(8,128)} fusion(f32[9000]{0:T(1024)} %param.9), kind=kLoop, calls=%fused_computation.2 | loop fusion | bytes 72864 | tf_op jit(solution)/shard_map/reshape | solution.py:188
  11.2 1.4 %pad_bitcast_fusion = (s32[72,128]{1,0:T(8,128)}, s32[72,128]{1,0:T(8,128)}) fusion(s32[9000]{0:T(1024)} %param.11, s32[9000]{0:T(1024)} %param.10), kind=kLoop, calls=%fused_computation | loop fusion | bytes 145728 | tf_op jit(solution)/shard_map/reshape | solution.py:190
  12.6 6.7 %add_weirs.1.a_ref = f32[2,512,512]{2,1,0:T(8,128)} custom-call(s32[16,16]{1,0:T(8,128)} %mask_ref.1, f32[2,512,512]{2,1,0:T(8,128)} %bitcast.12, f32[64,128]{1,0:T(8,128)} %gather_heads.1.heads_ref, f32[72,128]{1,0:T(8,128)} %pad_bitcast_fusion.2.coef_ref, s32[72,128]{1,0:T(8,128)} %get-tuple-element.6.node_ref, s32[72,128]{1,0:T(8,128)} %get-tuple-element.5.cell_ref), custom_call_target="tpu_custom_call" | custom-call | tf_op jit(solution)/shard_map/add_weirs/pallas_call | solution.py:192
  19.3 95.8 %eliminate.1 = f32[2,512,512]{2,1,0:T(8,128)} custom-call(f32[2,512,512]{2,1,0:T(8,128)} %add_weirs.1.a_ref), custom_call_target="tpu_custom_call" | custom-call | tf_op jit(solution)/shard_map/eliminate/pallas_call | solution.py:739
  115.1 3.1 %copy.9 = f32[1,1,2,1,512,512]{5,4,3,2,1,0:T(8,128)} copy(f32[1,1,2,1,512,512]{5,4,3,2,1,0:T(8,128)} %bitcast.11) | data formatting | bytes 4194304
